TPU v7x, 32 devices: a whole 2x2x4 slice. The times are simulated.
32 devices in a mesh: rows: 8 (over y, x, core), cols: 4 (over z).
Axes of the slice: x: 2, y: 2, z: 4, core: 2. Of those that a mesh axis runs over, the one named last changes fastest.
Arguments:
- feat_left: bfloat16 [128, 1024, 256], P('rows', 'cols'), may hold values from -6 to 6
- feat_right: bfloat16 [128, 1024, 256], P('rows', 'cols'), may hold values from -6 to 6
- hidden: bfloat16 [128, 1024, 128], P('rows', 'cols'), may hold values from -1 to 1
- disparity: int32 [128, 1024], P('rows', 'cols'), may hold values from 0 to 127
- motion_weight: bfloat16 [9, 128], replicated, may hold values from -2 to 2
- gate_weight: bfloat16 [3, 3, 256, 256], replicated, may hold values from -0.125 to 0.125
- cand_weight: bfloat16 [3, 3, 256, 128], replicated, may hold values from -0.125 to 0.125
- grad_hidden: bfloat16 [128, 1024, 128], P('rows', 'cols'), may hold values from -6 to 6
Outputs:
- new_hidden: bfloat16 [128, 1024, 128], P('rows', 'cols')
- grad_left: bfloat16 [128, 1024, 256], P('rows', 'cols')
- grad_right: bfloat16 [128, 1024, 256], P('rows', 'cols')
Inputs may be any that keep to these rules, and one draw needn't show every extreme that they name: Whole disparity levels.
All inputs are finite; a program needn't handle non-finite values.
Results may differ from a plain program's by a relative error of at most 0.0075.
Values may be sent and summed in bfloat16 or wider, within the bound.
A program may use at most 192 MiB of HBM per device.

v0:
```python
import math

import jax
import jax.numpy as jnp
from jax import lax
from jax.sharding import PartitionSpec as P

DISP = 128


def from_behind(array, axis, by):
    size = lax.axis_size(axis)
    pairs = [(i, i + by) for i in range(size) if 0 <= i + by < size]
    return lax.ppermute(array, axis, pairs)


def padded_2(block, sides, width):
    for axis, dim in sides:
        count = lax.axis_size(axis)
        forward = [(i, i + 1) for i in range(count - 1)]
        backward = [(target, source) for source, target in forward]
        low = lax.ppermute(
            lax.slice_in_dim(block, block.shape[dim] - width, None, axis=dim), axis, forward
        )
        high = lax.ppermute(lax.slice_in_dim(block, 0, width, axis=dim), axis, backward)
        block = jnp.concatenate([low, block, high], axis=dim)
    return block


def band_windows(own_right, before):
    row_count, col_count, chan_count = own_right.shape
    band_size = before.shape[1]
    extended = jnp.concatenate([before, own_right], axis=1)
    blocks = extended.reshape(row_count, col_count // band_size + 1, band_size, chan_count)
    return jnp.concatenate([blocks[:, :-1], blocks[:, 1:]], axis=2)


def tap_index(disparity, band_size, radius):
    col_count = disparity.shape[1]
    inner = jnp.arange(col_count, dtype=jnp.int32) % band_size
    offsets = jnp.arange(2 * radius + 1, dtype=jnp.int32) - radius
    levels = disparity[:, :, None] + offsets[None, None, :]
    usable = (levels >= 0) & (levels < band_size)
    columns = jnp.clip(inner[None, :, None] + band_size - levels, 0, 2 * band_size - 1)
    return (columns, usable)


def conv_local(padded, weight, row_count, col_count):
    result = None
    for row_off in range(3):
        for col_off in range(3):
            product_term = jnp.einsum(
                "hwi,io->hwo",
                padded[row_off : row_off + row_count, col_off : col_off + col_count],
                weight[row_off, col_off],
                preferred_element_type=jnp.float32,
            )
            result = product_term if result is None else result + product_term
    return result


def flipped(weight):
    return jnp.transpose(weight[::-1, ::-1], (0, 1, 3, 2))


def per_device(
    feat_left, feat_right, hidden, disparity, motion_weight, gate_weight, cand_weight, grad_hidden
):
    row_count, col_count, chan_count = feat_left.shape
    hidden_units = hidden.shape[2]
    band_size = DISP
    radius = motion_weight.shape[0] // 2
    scale = 1.0 / math.sqrt(chan_count)
    block_count = col_count // band_size
    previous = from_behind(feat_right, "cols", 1)
    before = previous[:, col_count - band_size :]
    windows = band_windows(feat_right, before)
    left_blocks = feat_left.reshape(row_count, block_count, band_size, chan_count)
    scores = (
        jnp.einsum("hbic,hbjc->hbij", left_blocks, windows, preferred_element_type=jnp.float32)
        * scale
    )
    columns, usable = tap_index(disparity, band_size, radius)
    positions = jnp.arange(2 * band_size, dtype=jnp.int32)
    flat_scores = scores.reshape(row_count, col_count, 2 * band_size)
    picked = []
    for tap in range(2 * radius + 1):
        picked.append(
            jnp.sum(jnp.where(columns[:, :, tap : tap + 1] == positions, flat_scores, 0.0), axis=2)
        )
    taps = jnp.stack(picked, axis=2)
    taps = jnp.where(usable, taps, 0.0).astype(jnp.bfloat16)
    motion_pre = jnp.einsum("hwk,km->hwm", taps, motion_weight, preferred_element_type=jnp.float32)
    motion = jax.nn.silu(motion_pre).astype(jnp.bfloat16)
    inputs = jnp.concatenate([hidden, motion], axis=2)
    padded_inputs = padded_2(inputs, (("rows", 0), ("cols", 1)), 1)
    gates = conv_local(padded_inputs, gate_weight, row_count, col_count)
    update = jax.nn.sigmoid(gates[..., :hidden_units])
    reset = jax.nn.sigmoid(gates[..., hidden_units:])
    hidden_f = hidden.astype(jnp.float32)
    reset_state = (reset * hidden_f).astype(jnp.bfloat16)
    padded_reset = padded_2(reset_state, (("rows", 0), ("cols", 1)), 1)
    cand_in = jnp.concatenate([padded_reset, padded_inputs[:, :, hidden_units:]], axis=2)
    cand = jnp.tanh(conv_local(cand_in, cand_weight, row_count, col_count))
    new_hidden = ((1.0 - update) * hidden_f + update * cand).astype(jnp.bfloat16)
    cotangent = grad_hidden.astype(jnp.float32)
    cand_grad = (cotangent * update * (1.0 - cand * cand)).astype(jnp.bfloat16)
    update_grad = cotangent * (cand - hidden_f) * update * (1.0 - update)
    padded_cand = padded_2(cand_grad, (("rows", 0), ("cols", 1)), 1)
    cand_back = conv_local(padded_cand, flipped(cand_weight), row_count, col_count)
    reset_grad = cand_back[..., :hidden_units] * hidden_f * reset * (1.0 - reset)
    gate_grads = jnp.concatenate([update_grad, reset_grad], axis=2).astype(jnp.bfloat16)
    padded_gates = padded_2(gate_grads, (("rows", 0), ("cols", 1)), 1)
    gate_back = conv_local(padded_gates, flipped(gate_weight), row_count, col_count)
    motion_grad = cand_back[..., hidden_units:] + gate_back[..., hidden_units:]
    sigmas = jax.nn.sigmoid(motion_pre)
    pre_grad = (motion_grad * sigmas * (1.0 + motion_pre * (1.0 - sigmas))).astype(jnp.bfloat16)
    tap_grad = jnp.einsum(
        "hwm,km->hwk", pre_grad, motion_weight, preferred_element_type=jnp.float32
    )
    tap_grad = jnp.where(usable, tap_grad, 0.0)
    score_grad = jnp.zeros((row_count, col_count, 2 * band_size), jnp.float32)
    for tap in range(2 * radius + 1):
        score_grad = score_grad + jnp.where(
            columns[:, :, tap : tap + 1] == positions, tap_grad[:, :, tap : tap + 1], 0.0
        )
    score_grad = score_grad.astype(jnp.bfloat16).reshape(
        row_count, block_count, band_size, 2 * band_size
    )
    grad_left = (
        (
            jnp.einsum("hbij,hbjc->hbic", score_grad, windows, preferred_element_type=jnp.float32)
            * scale
        )
        .reshape(row_count, col_count, chan_count)
        .astype(jnp.bfloat16)
    )
    window_grad = (
        jnp.einsum("hbij,hbic->hbjc", score_grad, left_blocks, preferred_element_type=jnp.float32)
        * scale
    )
    far_part = window_grad[:, :, :band_size].astype(jnp.bfloat16)
    incoming = from_behind(far_part[:, 0], "cols", -1)
    following = jnp.concatenate([far_part[:, 1:], incoming[:, None]], axis=1).astype(jnp.float32)
    grad_right = (
        (window_grad[:, :, band_size:] + following)
        .reshape(row_count, col_count, chan_count)
        .astype(jnp.bfloat16)
    )
    return (new_hidden, grad_left, grad_right)


def solution(mesh):
    return jax.shard_map(
        per_device,
        mesh=mesh,
        in_specs=(
            P("rows", "cols", None),
            P("rows", "cols", None),
            P("rows", "cols", None),
            P("rows", "cols"),
            P(),
            P(),
            P(),
            P("rows", "cols", None),
        ),
        out_specs=(P("rows", "cols", None), P("rows", "cols", None), P("rows", "cols", None)),
        check_vma=False,
    )
```

profile of v0, /device:TPU:11, one launch (start us, length us, event | category | flops | bytes accessed | tf_op | source)
XLA Modules:
  0.0 331.2 jit_solution(15061047384724104681)
XLA Ops:
  0.7 3.3 %collective-permute-start = (bf16[16,256,256]{2,1,0:T(8,128)(2,1)}, bf16[16,256,256]{2,1,0:T(8,128)(2,1)}, u32[]{:S(2)}, u32[]{:S(2)}) collective-permute-start(bf16[16,256,256]{2,1,0:T(8,128)(2,1)} %param.9), channel_id=1, source_target_pairs={{0,1},{1,2},{2,3},{4,5},{5,6},{6,7},{8,9},{9,10},{10,11},{12,13},{... | collective-permute-start | bytes 6291464 | tf_op jit(solution)/shard_map/ppermute | solution.py:14
  5.5 2.4 copy.182
  8.3 41.2 %collective-permute-done = bf16[16,256,256]{2,1,0:T(8,128)(2,1)} collective-permute-done((bf16[16,256,256]{2,1,0:T(8,128)(2,1)}, bf16[16,256,256]{2,1,0:T(8,128)(2,1)}, u32[]{:S(2)}, u32[]{:S(2)}) %collective-permute-start) | collective-permute-done | bytes 2097184 | tf_op jit(solution)/shard_map/ppermute | solution.py:14
  51.8 6.6 %fusion.14 = (f32[16,2,128]{2,1,0:T(2,128)S(1)}, f32[16,2,128]{2,1,0:T(2,128)S(1)}, f32[16,2,128]{2,1,0:T(2,128)S(1)}, f32[16,2,128]{2,1,0:T(2,128)S(1)}, f32[16...) fusion(s32[16,2,128]{2,1,0:T(2,128)S(1)} %bitcast.270, ...), kind=kOutput, calls=%fused_computation.26 | convolution fusion | flops 574582784 | bytes 6586368 | tf_op jit(solution)/shard_map/hbic,hbjc->hbij/dot_general | solution.py:80
  60.7 4.6 %collective-permute-start.1 = (bf16[1,256,256]{1,2,0:T(8,128)(2,1)S(1)}, bf16[1,256,256]{1,2,0:T(8,128)(2,1)S(1)}, u32[]{:S(2)}, u32[]{:S(2)}) collective-permute-start(bf16[1,256,256]{1,2,0:T(8,128)(2,1)S(1)} %get-tuple-element.38), channel_id=1, source_target_pairs={{0,4},{4,8},{8,12},{12,16},{16,20},{20,24},{24,28},{1,5},{5,9},{9,... | collective-permute-start | bytes 393224 | tf_op jit(solution)/shard_map/ppermute | solution.py:22
  67.2 3.7 %fusion.111 = f32[16,256,256]{1,2,0:T(8,128)} fusion(bf16[16,256,128]{1,2,0:T(8,128)(2,1)S(1)} %get-tuple-element.68, bf16[16,256,128]{1,2,0:T(8,128)(2,1)S(1)} %copy.118, bf16[3,3,256,256]{3,2,1,0:T(8,128)(2,1)} %param.13), kind=kOutput, calls=%fused_computation.157 | convolution fusion | flops 541065216 | bytes 6422528 | tf_op jit(solution)/shard_map/hwi,io->hwo/dot_general | solution.py:52
  76.4 3.2 collective-permute-start.3
  81.4 2.7 collective-permute-start.4
  84.1 4.0 %fusion.23 = f32[16,256,256]{1,2,0:T(8,128)} fusion(bf16[16,256,128]{1,2,0:T(8,128)(2,1)} %copy-done.10, bf16[16,256,128]{1,2,0:T(8,128)(2,1)S(1)} %copy.118, bf16[1,256,256]{1,2,0:T(8,128)(2,1)S(1)} %collective-permute-done.1, bf16[3,3,256,256]{3,2,1,0:T(8,128)(2,1)} %param.13), kind=kOutput, calls=%fused_computation.63 | convolution fusion | flops 543555584 | bytes 6553600 | tf_op jit(solution)/shard_map/hwi,io->hwo/dot_general | solution.py:52
  88.1 3.7 %fusion.29 = f32[16,256,256]{1,2,0:T(8,128)} fusion(bf16[1,256,256]{1,2,0:T(8,128)(2,1)S(1)} %collective-permute-done.2, bf16[16,256,128]{1,2,0:T(8,128)(2,1)S(1)} %copy-done.11, bf16[16,256,128]{1,2,0:T(8,128)(2,1)S(1)} %copy.118, bf16[3,3,256,256]{3,2,1,0:T(8,128)(2,1)} %param.13), kind=kOutput, calls=%fused_computation.69 | convolution fusion | flops 543555584 | bytes 6553600 | tf_op jit(solution)/shard_map/hwi,io->hwo/dot_general | solution.py:52
  94.7 6.1 %pad_maximum_fusion.1 = (bf16[18,257,256]{1,2,0:T(8,128)(2,1)S(1)}, bf16[18,257,256]{1,2,0:T(8,128)(2,1)S(1)}) fusion(bf16[18,1,256]{1,2,0:T(8,128)(2,1)} %copy.126, bf16[1,256,256]{1,2,0:T(8,128)(2,1)S(1)} %collective-permute-done.2, bf16[16,256,128]{1,2,0:T(8,128)(2,1)} %copy-done.10, bf16[16,256,128]{1,2,0:T(8,128)(2,1)S(1)} %copy.118, ...), kind=kLoop, calls=%fused_computation.53 | loop fusion | flops 23685120 | bytes 7114752 | tf_op jit(solution)/shard_map/concatenate | solution.py:26
  100.9 2.7 fusion.101
  103.6 2.8 fusion.105
  106.4 3.0 fusion.103
  109.4 3.0 fusion.107
  112.4 2.7 fusion.109
  115.1 12.1 %add_add_fusion.2 = f32[16,256,256]{1,2,0:T(8,128)S(1)} fusion(f32[16,256,256]{1,2,0:T(8,128)} %fusion.29, f32[16,256,256]{1,2,0:T(8,128)} %fusion.101, f32[16,256,256]{1,2,0:T(8,128)} %fusion.103, f32[16,256,256]{1,2,0:T(8,128)} %fusion.111, f32[16,256,256]{1,2,0:T(8,128)} %fusion.105, f32[16,256,256]{1,2,0:T(8,128)} %fusion.107, ...), kind=kOutput, calls=%fused_computation.32 | convolution fusion | flops 545259520 | bytes 39976960 | tf_op jit(solution)/shard_map/hwi,io->hwo/dot_general | solution.py:52
  127.9 3.7 %collective-permute-start.5 = (bf16[1,256,128]{1,2,0:T(8,128)(2,1)S(1)}, bf16[1,256,128]{1,2,0:T(8,128)(2,1)S(1)}, u32[]{:S(2)}, u32[]{:S(2)}) collective-permute-start(bf16[1,256,128]{1,2,0:T(8,128)(2,1)S(1)} %get-tuple-element.48), channel_id=1, source_target_pairs={{0,4},{4,8},{8,12},{12,16},{16,20},{20,24},{24,28},{1,5},{5,9},{9,... | collective-permute-start | bytes 196616 | tf_op jit(solution)/shard_map/ppermute | solution.py:22
  134.6 3.4 %collective-permute-done.6 = bf16[1,256,128]{1,2,0:T(8,128)(2,1)S(1)} collective-permute-done((bf16[1,256,128]{1,2,0:T(8,128)(2,1)S(1)}, bf16[1,256,128]{1,2,0:T(8,128)(2,1)S(1)}, u32[]{:S(2)}, u32[]{:S(2)}) %collective-permute-start.6) | collective-permute-done | bytes 65568 | tf_op jit(solution)/shard_map/ppermute | solution.py:25
  141.4 3.2 collective-permute-start.7
  146.6 2.8 collective-permute-start.8
  157.2 5.8 %fusion.17 = bf16[18,258,256]{1,2,0:T(8,128)(2,1)S(1)} fusion(bf16[18,1,256]{1,2,0:T(8,128)(2,1)} %copy.126, bf16[18,1,256]{1,2,0:T(8,128)(2,1)} %copy.120, bf16[1,256,256]{1,2,0:T(8,128)(2,1)S(1)} %collective-permute-done.2, bf16[1,256,256]{1,2,0:T(8,128)(2,1)S(1)} %collective-permute-done.1, bf16[16,256,128]{1,2,0:T(8,128)(2,1)} %copy-done.10, ...), kind=kLoop, calls=%fused_computation.48 | loop fusion | flops 33288192 | bytes 5944320 | tf_op jit(solution)/shard_map/concatenate | solution.py:103
  171.9 5.5 %fusion.51 = (bf16[16,256,128]{1,2,0:T(8,128)(2,1)}, bf16[16,256,128]{1,2,0:T(8,128)(2,1)}, bf16[16,256,128]{1,2,0:T(8,128)(2,1)S(1)}) fusion(bf16[16,256,128]{1,2,0:T(8,128)(2,1)S(1)} %copy-done.19, bf16[16,256,128]{1,2,0:T(8,128)(2,1)S(1)} %copy.118, f32[16,256,256]{1,2,0:T(8,128)S(1)} %copy-done.4, bf16[3,3,256,128]{3,2,1,0:T(8,128)(2,1)} %param.14, ...), kind=kOutput, calls=%fused_computation.91 | convolution fusion | flops 283115520 | bytes 26279936 | tf_op jit(solution)/shard_map/hwi,io->hwo/dot_general | solution.py:52
  181.8 3.5 %fusion.161 = f32[16,256,256]{1,2,0:T(8,128)} fusion(bf16[16,256,128]{1,2,0:T(8,128)(2,1)S(1)} %get-tuple-element.23, bf16[3,3,128,256]{2,3,1,0:T(8,128)(2,1)} %reverse_bitcast_fusion.1), kind=kOutput, calls=%fused_computation.239 | convolution fusion | flops 268435456 | bytes 5308416 | tf_op jit(solution)/shard_map/hwi,io->hwo/dot_general | solution.py:52
  191.6 2.6 collective-permute-start.11
  195.6 3.0 collective-permute-start.12
  198.6 3.9 %fusion.133 = f32[16,256,256]{1,2,0:T(8,128)} fusion(bf16[16,256,128]{1,2,0:T(8,128)(2,1)} %copy-done.1, bf16[1,256,128]{1,2,0:T(8,128)(2,1)S(1)} %collective-permute-done.9, bf16[3,3,128,256]{2,3,1,0:T(8,128)(2,1)} %reverse_bitcast_fusion.1), kind=kOutput, calls=%fused_computation.190 | convolution fusion | flops 270532608 | bytes 5373952 | tf_op jit(solution)/shard_map/hwi,io->hwo/dot_general | solution.py:52
  202.5 3.6 %fusion.123 = f32[16,256,256]{1,2,0:T(8,128)} fusion(bf16[1,256,128]{1,2,0:T(8,128)(2,1)S(1)} %collective-permute-done.10, bf16[16,256,128]{1,2,0:T(8,128)(2,1)S(1)} %copy-done.2, bf16[3,3,128,256]{2,3,1,0:T(8,128)(2,1)} %reverse_bitcast_fusion.1), kind=kOutput, calls=%fused_computation.179 | convolution fusion | flops 270532608 | bytes 5373952 | tf_op jit(solution)/shard_map/hwi,io->hwo/dot_general | solution.py:52
  208.4 2.9 pad_maximum_fusion.10
  211.2 2.8 fusion.127
  214.1 2.8 fusion.131
  216.8 2.8 fusion.129
  219.6 2.8 fusion.135
  222.4 2.7 fusion.125
  225.9 13.2 %add_add_fusion.1 = f32[16,256,256]{1,2,0:T(8,128)} fusion(f32[16,256,256]{1,2,0:T(8,128)} %fusion.123, f32[16,256,256]{1,2,0:T(8,128)} %fusion.125, f32[16,256,256]{1,2,0:T(8,128)} %fusion.127, f32[16,256,256]{1,2,0:T(8,128)S(1)} %copy-done.12, f32[16,256,256]{1,2,0:T(8,128)} %fusion.129, f32[16,256,256]{1,2,0:T(8,128)} %fusion.131, ...), kind=kOutput, calls=%fused_computation.31 | convolution fusion | flops 276824064 | bytes 38862848 | tf_op jit(solution)/shard_map/hwi,io->hwo/dot_general | solution.py:52
  241.6 5.1 %collective-permute-start.13 = (bf16[1,256,256]{1,2,0:T(8,128)(2,1)S(1)}, bf16[1,256,256]{1,2,0:T(8,128)(2,1)S(1)}, u32[]{:S(2)}, u32[]{:S(2)}) collective-permute-start(bf16[1,256,256]{1,2,0:T(8,128)(2,1)S(1)} %get-tuple-element.36), channel_id=1, source_target_pairs={{0,4},{4,8},{8,12},{12,16},{16,20},{20,24},{24,28},{1,5},{5,9},{9,... | collective-permute-start | bytes 393224 | tf_op jit(solution)/shard_map/ppermute | solution.py:22
  248.6 3.7 %fusion.115 = f32[16,256,256]{1,2,0:T(8,128)} fusion(bf16[16,256,128]{1,2,0:T(8,128)(2,1)S(1)} %fusion.57, bf16[16,256,128]{1,2,0:T(8,128)(2,1)S(1)} %copy-done.6, bf16[3,3,256,256]{3,2,1,0:T(8,128)(2,1)} %reverse_bitcast_fusion), kind=kOutput, calls=%fused_computation.161 | convolution fusion | flops 541065216 | bytes 6422528 | tf_op jit(solution)/shard_map/hwi,io->hwo/dot_general | solution.py:52
  257.9 2.8 collective-permute-start.15
  262.5 2.9 collective-permute-start.16
  265.4 3.9 %fusion.35 = f32[16,256,256]{1,2,0:T(8,128)} fusion(bf16[16,256,128]{1,2,0:T(8,128)(2,1)} %copy-done.8, bf16[16,256,128]{1,2,0:T(8,128)(2,1)S(1)} %copy-done.7, bf16[1,256,256]{1,2,0:T(8,128)(2,1)S(1)} %collective-permute-done.13, bf16[3,3,256,256]{3,2,1,0:T(8,128)(2,1)} %reverse_bitcast_fusion), kind=kOutput, calls=%fused_computation.75 | convolution fusion | flops 543555584 | bytes 6553600 | tf_op jit(solution)/shard_map/hwi,io->hwo/dot_general | solution.py:52
  269.3 3.7 %fusion.41 = f32[16,256,256]{1,2,0:T(8,128)} fusion(bf16[1,256,256]{1,2,0:T(8,128)(2,1)S(1)} %collective-permute-done.14, bf16[16,256,128]{1,2,0:T(8,128)(2,1)S(1)} %copy-done.9, bf16[16,256,128]{1,2,0:T(8,128)(2,1)S(1)} %copy-done.7, bf16[3,3,256,256]{3,2,1,0:T(8,128)(2,1)} %reverse_bitcast_fusion), kind=kOutput, calls=%fused_computation.81 | convolution fusion | flops 543555584 | bytes 6553600 | tf_op jit(solution)/shard_map/hwi,io->hwo/dot_general | solution.py:52
  276.0 6.1 %maximum_maximum_fusion.1 = (bf16[18,257,256]{1,2,0:T(8,128)(2,1)S(1)}, bf16[18,257,256]{1,2,0:T(8,128)(2,1)S(1)}) fusion(bf16[1,256,256]{1,2,0:T(8,128)(2,1)S(1)} %collective-permute-done.14, bf16[16,256,128]{1,2,0:T(8,128)(2,1)} %copy-done.8, bf16[16,256,128]{1,2,0:T(8,128)(2,1)S(1)} %copy-done.7, bf16[1,256,256]{1,2,0:T(8,128)(2,1)S(1)} %collective-permute-done.13, ...), kind=kLoop, calls=%fused_computation.54 | loop fusion | flops 23685120 | bytes 7114752 | tf_op jit(solution)/shard_map/concatenate | solution.py:26
  285.7 2.8 fusion.68
  288.5 3.8 %add_add_fusion = f32[16,256,256]{1,2,0:T(8,128)S(1)} fusion(f32[16,256,256]{1,2,0:T(8,128)S(1)} %fusion.71, f32[16,256,256]{1,2,0:T(8,128)} %fusion.35, bf16[18,257,256]{1,2,0:T(8,128)(2,1)S(1)} %get-tuple-element.29, bf16[3,3,256,256]{3,2,1,0:T(8,128)(2,1)S(1)} %copy-done.21), kind=kOutput, calls=%fused_computation.30 | convolution fusion | flops 538968064 | bytes 14811136 | tf_op jit(solution)/shard_map/hwi,io->hwo/dot_general | solution.py:52
  293.3 3.8 %convolution_select_fusion = f32[16,256,9]{1,2,0:T(8,128)S(1)} fusion(f32[16,256,256]{1,2,0:T(8,128)S(1)} %fusion.62, f32[16,256,256]{1,2,0:T(8,128)} %fusion.41, f32[16,256,256]{1,2,0:T(8,128)S(1)} %fusion.64, f32[16,256,256]{1,2,0:T(8,128)S(1)} %fusion.66, f32[16,256,256]{1,2,0:T(8,128)S(1)} %copy-done.17, f32[16,256,256]{1,2,0:T(8,128)} %fusion.68, ...), kind=kOutput, calls=%fused_computation.173 | convolution fusion | flops 18010112 | bytes 19042816 | tf_op jit(solution)/shard_map/hwm,km->hwk/dot_general | solution.py:118
  297.3 5.4 %fusion.210 = (bf16[16,2,256,256]{3,2,1,0:T(8,128)(2,1)S(1)}, f32[16,2,256,256]{3,2,1,0:T(8,128)S(1)}) fusion(bf16[16,2,128,256]{3,2,1,0:T(8,128)(2,1)S(1)} %bitcast.263, f32[16,2,128]{2,1,0:T(2,128)S(1)} %bitcast.296, f32[16,2,128]{2,1,0:T(2,128)S(1)} %bitcast.298, f32[16,2,128]{2,1,0:T(2,128)S(1)} %bitcast.300, f32[16,2,128]{2,1,0:T(2,128)S(1)} %bitcast.302, ...), kind=kOutput, calls=%fused_computation.290 | convolution fusion | flops 569376768 | bytes 14974976 | tf_op jit(solution)/shard_map/hbij,hbic->hbjc/dot_general | solution.py:139
  305.1 6.3 %multiply_convert_fusion = bf16[16,2,128,256]{3,2,1,0:T(8,128)(2,1)} fusion(bf16[16,2,128,256]{3,2,1,0:T(8,128)(2,1)S(1)} %copy-done.28, bf16[16,2,128,256]{3,2,1,0:T(8,128)(2,1)S(1)} %copy-done.26, f32[16,2,128]{2,1,0:T(2,128)S(1)} %bitcast.297, f32[16,2,128]{2,1,0:T(2,128)S(1)} %bitcast.299, f32[16,2,128]{2,1,0:T(2,128)S(1)} %bitcast.301, ...), kind=kOutput, calls=%fused_computation.28 | convolution fusion | flops 575668224 | bytes 6586368 | tf_op jit(solution)/shard_map/hbij,hbjc->hbic/dot_general | solution.py:132
  311.4 17.1 %collective-permute-done.17 = bf16[16,128,256]{2,1,0:T(8,128)(2,1)S(1)} collective-permute-done((bf16[16,128,256]{2,1,0:T(8,128)(2,1)S(1)}, bf16[16,128,256]{2,1,0:T(8,128)(2,1)S(1)}, u32[]{:S(2)}, u32[]{:S(2)}) %collective-permute-start.17) | collective-permute-done | bytes 1048608 | tf_op jit(solution)/shard_map/ppermute | solution.py:14
  (185 shorter events, 83.2 us)
Async XLA Ops:
  0.6 51.1 %copy-start = (bf16[16,256,256]{2,1,0:T(8,128)(2,1)S(1)}, bf16[16,256,256]{2,1,0:T(8,128)(2,1)}, u32[]{:S(2)}) copy-start(bf16[16,256,256]{2,1,0:T(8,128)(2,1)} %param.8) | copy-start | bytes 6291460
  0.6 7.3 %copy-start.29 = (s32[16,256]{1,0:T(8,128)S(1)}, s32[16,256]{1,0:T(8,128)}, u32[]{:S(2)}) copy-start(s32[16,256]{1,0:T(8,128)} %param.11) | copy-start | bytes 49156
  0.7 48.8 %collective-permute-start = (bf16[16,256,256]{2,1,0:T(8,128)(2,1)}, bf16[16,256,256]{2,1,0:T(8,128)(2,1)}, u32[]{:S(2)}, u32[]{:S(2)}) collective-permute-start(bf16[16,256,256]{2,1,0:T(8,128)(2,1)} %param.9), channel_id=1, source_target_pairs={{0,1},{1,2},{2,3},{4,5},{5,6},{6,7},{8,9},{9,10},{10,11},{12,13},{... | collective-permute-start | bytes 6291464 | tf_op jit(solution)/shard_map/ppermute | solution.py:14
  7.9 42.9 %copy-start.24 = (bf16[16,256,256]{2,1,0:T(8,128)(2,1)S(1)}, bf16[16,256,256]{2,1,0:T(8,128)(2,1)}, u32[]{:S(2)}) copy-start(bf16[16,256,256]{2,1,0:T(8,128)(2,1)} %param.9) | copy-start | bytes 6291460
  7.9 50.7 %copy-start.50 = (s32[9]{0:T(128)}, s32[9]{0:T(128)S(1)}, u32[]{:S(2)}) copy-start(s32[9]{0:T(128)S(1)} %iota_add_fusion) | copy-start | bytes 112
  8.2 43.5 %copy-start.30 = (s32[16,256,1]{1,2,0:T(1,128)}, s32[16,256,1]{1,2,0:T(1,128)S(1)}, u32[]{:S(2)}) copy-start(s32[16,256,1]{1,2,0:T(1,128)S(1)} %get-tuple-element.59) | copy-start | bytes 49156
  8.2 43.5 %copy-start.32 = (s32[16,256,1]{1,2,0:T(1,128)}, s32[16,256,1]{1,2,0:T(1,128)S(1)}, u32[]{:S(2)}) copy-start(s32[16,256,1]{1,2,0:T(1,128)S(1)} %get-tuple-element.60) | copy-start | bytes 49156
  8.2 43.5 %copy-start.34 = (s32[16,256,1]{1,2,0:T(1,128)}, s32[16,256,1]{1,2,0:T(1,128)S(1)}, u32[]{:S(2)}) copy-start(s32[16,256,1]{1,2,0:T(1,128)S(1)} %get-tuple-element.61) | copy-start | bytes 49156
  8.2 43.5 %copy-start.36 = (s32[16,256,1]{1,2,0:T(1,128)}, s32[16,256,1]{1,2,0:T(1,128)S(1)}, u32[]{:S(2)}) copy-start(s32[16,256,1]{1,2,0:T(1,128)S(1)} %get-tuple-element.62) | copy-start | bytes 49156
  8.2 43.5 %copy-start.38 = (s32[16,256,1]{1,2,0:T(1,128)}, s32[16,256,1]{1,2,0:T(1,128)S(1)}, u32[]{:S(2)}) copy-start(s32[16,256,1]{1,2,0:T(1,128)S(1)} %get-tuple-element.63) | copy-start | bytes 49156
  8.3 43.5 %copy-start.40 = (s32[16,256,1]{1,2,0:T(1,128)}, s32[16,256,1]{1,2,0:T(1,128)S(1)}, u32[]{:S(2)}) copy-start(s32[16,256,1]{1,2,0:T(1,128)S(1)} %get-tuple-element.64) | copy-start | bytes 49156
  8.3 43.5 %copy-start.42 = (s32[16,256,1]{1,2,0:T(1,128)}, s32[16,256,1]{1,2,0:T(1,128)S(1)}, u32[]{:S(2)}) copy-start(s32[16,256,1]{1,2,0:T(1,128)S(1)} %get-tuple-element.65) | copy-start | bytes 49156
  8.3 43.5 %copy-start.44 = (s32[16,256,1]{1,2,0:T(1,128)}, s32[16,256,1]{1,2,0:T(1,128)S(1)}, u32[]{:S(2)}) copy-start(s32[16,256,1]{1,2,0:T(1,128)S(1)} %get-tuple-element.66) | copy-start | bytes 49156
  8.3 43.5 %copy-start.46 = (s32[16,256,1]{1,2,0:T(1,128)}, s32[16,256,1]{1,2,0:T(1,128)S(1)}, u32[]{:S(2)}) copy-start(s32[16,256,1]{1,2,0:T(1,128)S(1)} %get-tuple-element.67) | copy-start | bytes 49156
  51.7 6.7 %copy-start.25 = (bf16[16,2,128,256]{3,2,1,0:T(8,128)(2,1)}, bf16[16,2,128,256]{3,2,1,0:T(8,128)(2,1)S(1)}, u32[]{:S(2)}) copy-start(bf16[16,2,128,256]{3,2,1,0:T(8,128)(2,1)S(1)} %get-tuple-element.26) | copy-start | bytes 6291460
  51.7 6.7 %copy-start.27 = (bf16[16,2,128,256]{3,2,1,0:T(8,128)(2,1)}, bf16[16,2,128,256]{3,2,1,0:T(8,128)(2,1)S(1)}, u32[]{:S(2)}) copy-start(bf16[16,2,128,256]{3,2,1,0:T(8,128)(2,1)S(1)} %get-tuple-element.27) | copy-start | bytes 6291460
  51.8 6.9 %copy-start.48 = (bf16[9,128]{1,0:T(8,128)(2,1)S(1)}, bf16[9,128]{1,0:T(8,128)(2,1)}, u32[]{:S(2)}) copy-start(bf16[9,128]{1,0:T(8,128)(2,1)} %param.12) | copy-start | bytes 6916
  60.7 11.8 %copy-start.10 = (bf16[16,256,128]{1,2,0:T(8,128)(2,1)}, bf16[16,256,128]{1,2,0:T(8,128)(2,1)S(1)}, u32[]{:S(2)}) copy-start(bf16[16,256,128]{1,2,0:T(8,128)(2,1)S(1)} %get-tuple-element.68) | copy-start | bytes 3145732
  60.7 10.2 %collective-permute-start.1 = (bf16[1,256,256]{1,2,0:T(8,128)(2,1)S(1)}, bf16[1,256,256]{1,2,0:T(8,128)(2,1)S(1)}, u32[]{:S(2)}, u32[]{:S(2)}) collective-permute-start(bf16[1,256,256]{1,2,0:T(8,128)(2,1)S(1)} %get-tuple-element.38), channel_id=1, source_target_pairs={{0,4},{4,8},{8,12},{12,16},{16,20},{20,24},{24,28},{1,5},{5,9},{9,... | collective-permute-start | bytes 393224 | tf_op jit(solution)/shard_map/ppermute | solution.py:22
  65.2 7.2 %collective-permute-start.2 = (bf16[1,256,256]{1,2,0:T(8,128)(2,1)S(1)}, bf16[1,256,256]{1,2,0:T(8,128)(2,1)S(1)}, u32[]{:S(2)}, u32[]{:S(2)}) collective-permute-start(bf16[1,256,256]{1,2,0:T(8,128)(2,1)S(1)} %get-tuple-element.39), channel_id=1, source_target_pairs={{4,0},{8,4},{12,8},{16,12},{20,16},{24,20},{28,24},{5,1},{9,5},{13... | collective-permute-start | bytes 393224 | tf_op jit(solution)/shard_map/ppermute | solution.py:25
  76.4 15.4 %collective-permute-start.3 = (bf16[18,1,256]{2,0,1:T(8,128)(2,1)S(1)}, bf16[18,1,256]{2,0,1:T(8,128)(2,1)S(1)}, u32[]{:S(2)}, u32[]{:S(2)}) collective-permute-start(bf16[18,1,256]{2,0,1:T(8,128)(2,1)S(1)} %copy.119), channel_id=1, source_target_pairs={{0,1},{1,2},{2,3},{4,5},{5,6},{6,7},{8,9},{9,10},{10,11},{12,13},{... | collective-permute-start | bytes 27656 | tf_op jit(solution)/shard_map/ppermute | solution.py:22
  81.4 6.7 %copy-start.11 = (bf16[16,256,128]{1,2,0:T(8,128)(2,1)S(1)}, bf16[16,256,128]{1,2,0:T(8,128)(2,1)}, u32[]{:S(2)}) copy-start(bf16[16,256,128]{1,2,0:T(8,128)(2,1)} %copy-done.10) | copy-start | bytes 3145732
  81.4 11.8 %collective-permute-start.4 = (bf16[18,1,256]{2,0,1:T(8,128)(2,1)S(1)}, bf16[18,1,256]{2,0,1:T(8,128)(2,1)S(1)}, u32[]{:S(2)}, u32[]{:S(2)}) collective-permute-start(bf16[18,1,256]{2,0,1:T(8,128)(2,1)S(1)} %copy.125), channel_id=1, source_target_pairs={{1,0},{2,1},{3,2},{5,4},{6,5},{7,6},{9,8},{10,9},{11,10},{13,12},{... | collective-permute-start | bytes 27656 | tf_op jit(solution)/shard_map/ppermute | solution.py:25
  94.7 6.2 %copy-start.20 = (bf16[3,3,256,256]{3,2,1,0:T(8,128)(2,1)S(1)}, bf16[3,3,256,256]{3,2,1,0:T(8,128)(2,1)}, u32[]{:S(2)}) copy-start(bf16[3,3,256,256]{3,2,1,0:T(8,128)(2,1)} %param.13) | copy-start | bytes 3538948
  127.2 10.9 %copy-start.3 = (f32[16,256,256]{1,2,0:T(8,128)}, f32[16,256,256]{1,2,0:T(8,128)S(1)}, u32[]{:S(2)}) copy-start(f32[16,256,256]{1,2,0:T(8,128)S(1)} %add_add_fusion.2) | copy-start | bytes 12582916
  127.2 6.2 %copy-start.18 = (bf16[3,3,256,256]{2,3,1,0:T(8,128)(2,1)S(1)}, bf16[3,3,256,256]{2,3,1,0:T(8,128)(2,1)}, u32[]{:S(2)}) copy-start(bf16[3,3,256,256]{2,3,1,0:T(8,128)(2,1)} %copy.182) | copy-start | bytes 3538948
  127.8 11.7 %copy-start.16 = (bf16[16,256,128]{1,2,0:T(8,128)(2,1)}, bf16[16,256,128]{1,2,0:T(8,128)(2,1)S(1)}, u32[]{:S(2)}) copy-start(bf16[16,256,128]{1,2,0:T(8,128)(2,1)S(1)} %fusion.54) | copy-start | bytes 3145732
  127.9 6.8 %collective-permute-start.5 = (bf16[1,256,128]{1,2,0:T(8,128)(2,1)S(1)}, bf16[1,256,128]{1,2,0:T(8,128)(2,1)S(1)}, u32[]{:S(2)}, u32[]{:S(2)}) collective-permute-start(bf16[1,256,128]{1,2,0:T(8,128)(2,1)S(1)} %get-tuple-element.48), channel_id=1, source_target_pairs={{0,4},{4,8},{8,12},{12,16},{16,20},{20,24},{24,28},{1,5},{5,9},{9,... | collective-permute-start | bytes 196616 | tf_op jit(solution)/shard_map/ppermute | solution.py:22
  131.5 6.5 %collective-permute-start.6 = (bf16[1,256,128]{1,2,0:T(8,128)(2,1)S(1)}, bf16[1,256,128]{1,2,0:T(8,128)(2,1)S(1)}, u32[]{:S(2)}, u32[]{:S(2)}) collective-permute-start(bf16[1,256,128]{1,2,0:T(8,128)(2,1)S(1)} %get-tuple-element.49), channel_id=1, source_target_pairs={{4,0},{8,4},{12,8},{16,12},{20,16},{24,20},{28,24},{5,1},{9,5},{13... | collective-permute-start | bytes 196616 | tf_op jit(solution)/shard_map/ppermute | solution.py:25
  141.4 12.2 %collective-permute-start.7 = (bf16[18,1,128]{2,0,1:T(8,128)(2,1)}, bf16[18,1,128]{2,0,1:T(8,128)(2,1)}, u32[]{:S(2)}, u32[]{:S(2)}) collective-permute-start(bf16[18,1,128]{2,0,1:T(8,128)(2,1)} %copy.142), channel_id=1, source_target_pairs={{0,1},{1,2},{2,3},{4,5},{5,6},{6,7},{8,9},{9,10},{10,11},{12,13},{... | collective-permute-start | bytes 13832 | tf_op jit(solution)/shard_map/ppermute | solution.py:22
  146.6 8.8 %collective-permute-start.8 = (bf16[18,1,128]{2,0,1:T(8,128)(2,1)}, bf16[18,1,128]{2,0,1:T(8,128)(2,1)}, u32[]{:S(2)}, u32[]{:S(2)}) collective-permute-start(bf16[18,1,128]{2,0,1:T(8,128)(2,1)} %copy.143), channel_id=1, source_target_pairs={{1,0},{2,1},{3,2},{5,4},{6,5},{7,6},{9,8},{10,9},{11,10},{13,12},{... | collective-permute-start | bytes 13832 | tf_op jit(solution)/shard_map/ppermute | solution.py:25
  157.2 5.8 %copy-start.22 = (bf16[3,3,256,128]{3,2,1,0:T(8,128)(2,1)S(1)}, bf16[3,3,256,128]{3,2,1,0:T(8,128)(2,1)}, u32[]{:S(2)}) copy-start(bf16[3,3,256,128]{3,2,1,0:T(8,128)(2,1)} %param.14) | copy-start | bytes 1769476
  177.4 10.2 %collective-permute-start.9 = (bf16[1,256,128]{1,2,0:T(8,128)(2,1)S(1)}, bf16[1,256,128]{1,2,0:T(8,128)(2,1)S(1)}, u32[]{:S(2)}, u32[]{:S(2)}) collective-permute-start(bf16[1,256,128]{1,2,0:T(8,128)(2,1)S(1)} %get-tuple-element.46), channel_id=1, source_target_pairs={{0,4},{4,8},{8,12},{12,16},{16,20},{20,24},{24,28},{1,5},{5,9},{9,... | collective-permute-start | bytes 196616 | tf_op jit(solution)/shard_map/ppermute | solution.py:22
  179.9 7.8 %collective-permute-start.10 = (bf16[1,256,128]{1,2,0:T(8,128)(2,1)S(1)}, bf16[1,256,128]{1,2,0:T(8,128)(2,1)S(1)}, u32[]{:S(2)}, u32[]{:S(2)}) collective-permute-start(bf16[1,256,128]{1,2,0:T(8,128)(2,1)S(1)} %get-tuple-element.47), channel_id=1, source_target_pairs={{4,0},{8,4},{12,8},{16,12},{20,16},{24,20},{28,24},{5,1},{9,5},{13... | collective-permute-start | bytes 196616 | tf_op jit(solution)/shard_map/ppermute | solution.py:25
  191.6 14.5 %collective-permute-start.11 = (bf16[18,1,128]{2,0,1:T(8,128)(2,1)S(1)}, bf16[18,1,128]{2,0,1:T(8,128)(2,1)S(1)}, u32[]{:S(2)}, u32[]{:S(2)}) collective-permute-start(bf16[18,1,128]{2,0,1:T(8,128)(2,1)S(1)} %copy.167), channel_id=1, source_target_pairs={{0,1},{1,2},{2,3},{4,5},{5,6},{6,7},{8,9},{9,10},{10,11},{12,13},{... | collective-permute-start | bytes 13832 | tf_op jit(solution)/shard_map/ppermute | solution.py:22
  195.6 6.9 %copy-start.2 = (bf16[16,256,128]{1,2,0:T(8,128)(2,1)S(1)}, bf16[16,256,128]{1,2,0:T(8,128)(2,1)}, u32[]{:S(2)}) copy-start(bf16[16,256,128]{1,2,0:T(8,128)(2,1)} %copy-done.1) | copy-start | bytes 3145732
  195.6 11.6 %collective-permute-start.12 = (bf16[18,1,128]{2,0,1:T(8,128)(2,1)S(1)}, bf16[18,1,128]{2,0,1:T(8,128)(2,1)S(1)}, u32[]{:S(2)}, u32[]{:S(2)}) collective-permute-start(bf16[18,1,128]{2,0,1:T(8,128)(2,1)S(1)} %copy.171), channel_id=1, source_target_pairs={{1,0},{2,1},{3,2},{5,4},{6,5},{7,6},{9,8},{10,9},{11,10},{13,12},{... | collective-permute-start | bytes 13832 | tf_op jit(solution)/shard_map/ppermute | solution.py:25
  211.2 5.6 %copy-start.15 = (bf16[18,257,128]{1,2,0:T(8,128)(2,1)}, bf16[18,257,128]{1,2,0:T(8,128)(2,1)S(1)}, u32[]{:S(2)}) copy-start(bf16[18,257,128]{1,2,0:T(8,128)(2,1)S(1)} %get-tuple-element.40) | copy-start | bytes 3552772
  225.9 13.2 %copy-start.5 = (f32[16,256,256]{1,2,0:T(8,128)S(1)}, f32[16,256,256]{1,2,0:T(8,128)}, u32[]{:S(2)}) copy-start(f32[16,256,256]{1,2,0:T(8,128)} %copy-done.3) | copy-start | bytes 12582916
  241.5 12.3 %copy-start.8 = (bf16[16,256,128]{1,2,0:T(8,128)(2,1)}, bf16[16,256,128]{1,2,0:T(8,128)(2,1)S(1)}, u32[]{:S(2)}) copy-start(bf16[16,256,128]{1,2,0:T(8,128)(2,1)S(1)} %fusion.57) | copy-start | bytes 3145732
  241.6 10.7 %collective-permute-start.13 = (bf16[1,256,256]{1,2,0:T(8,128)(2,1)S(1)}, bf16[1,256,256]{1,2,0:T(8,128)(2,1)S(1)}, u32[]{:S(2)}, u32[]{:S(2)}) collective-permute-start(bf16[1,256,256]{1,2,0:T(8,128)(2,1)S(1)} %get-tuple-element.36), channel_id=1, source_target_pairs={{0,4},{4,8},{8,12},{12,16},{16,20},{20,24},{24,28},{1,5},{5,9},{9,... | collective-permute-start | bytes 393224 | tf_op jit(solution)/shard_map/ppermute | solution.py:22
  246.7 7.2 %collective-permute-start.14 = (bf16[1,256,256]{1,2,0:T(8,128)(2,1)S(1)}, bf16[1,256,256]{1,2,0:T(8,128)(2,1)S(1)}, u32[]{:S(2)}, u32[]{:S(2)}) collective-permute-start(bf16[1,256,256]{1,2,0:T(8,128)(2,1)S(1)} %get-tuple-element.37), channel_id=1, source_target_pairs={{4,0},{8,4},{12,8},{16,12},{20,16},{24,20},{28,24},{5,1},{9,5},{13... | collective-permute-start | bytes 393224 | tf_op jit(solution)/shard_map/ppermute | solution.py:25
  254.1 11.3 %copy-start.7 = (bf16[16,256,128]{1,2,0:T(8,128)(2,1)S(1)}, bf16[16,256,128]{1,2,0:T(8,128)(2,1)}, u32[]{:S(2)}) copy-start(bf16[16,256,128]{1,2,0:T(8,128)(2,1)} %get-tuple-element.21) | copy-start | bytes 3145732
  257.9 15.1 %collective-permute-start.15 = (bf16[18,1,256]{2,0,1:T(8,128)(2,1)S(1)}, bf16[18,1,256]{2,0,1:T(8,128)(2,1)S(1)}, u32[]{:S(2)}, u32[]{:S(2)}) collective-permute-start(bf16[18,1,256]{2,0,1:T(8,128)(2,1)S(1)} %copy.180), channel_id=1, source_target_pairs={{0,1},{1,2},{2,3},{4,5},{5,6},{6,7},{8,9},{9,10},{10,11},{12,13},{... | collective-permute-start | bytes 27656 | tf_op jit(solution)/shard_map/ppermute | solution.py:22
  262.5 6.8 %copy-start.9 = (bf16[16,256,128]{1,2,0:T(8,128)(2,1)S(1)}, bf16[16,256,128]{1,2,0:T(8,128)(2,1)}, u32[]{:S(2)}) copy-start(bf16[16,256,128]{1,2,0:T(8,128)(2,1)} %copy-done.8) | copy-start | bytes 3145732
  262.5 12.0 %collective-permute-start.16 = (bf16[18,1,256]{2,0,1:T(8,128)(2,1)S(1)}, bf16[18,1,256]{2,0,1:T(8,128)(2,1)S(1)}, u32[]{:S(2)}, u32[]{:S(2)}) collective-permute-start(bf16[18,1,256]{2,0,1:T(8,128)(2,1)S(1)} %copy.187), channel_id=1, source_target_pairs={{1,0},{2,1},{3,2},{5,4},{6,5},{7,6},{9,8},{10,9},{11,10},{13,12},{... | collective-permute-start | bytes 27656 | tf_op jit(solution)/shard_map/ppermute | solution.py:25
  276.0 6.1 %copy-start.21 = (bf16[3,3,256,256]{3,2,1,0:T(8,128)(2,1)S(1)}, bf16[3,3,256,256]{3,2,1,0:T(8,128)(2,1)}, u32[]{:S(2)}) copy-start(bf16[3,3,256,256]{3,2,1,0:T(8,128)(2,1)} %reverse_bitcast_fusion) | copy-start | bytes 3538948
  302.9 25.6 %collective-permute-start.17 = (bf16[16,128,256]{2,1,0:T(8,128)(2,1)S(1)}, bf16[16,128,256]{2,1,0:T(8,128)(2,1)S(1)}, u32[]{:S(2)}, u32[]{:S(2)}) collective-permute-start(bf16[16,128,256]{2,1,0:T(8,128)(2,1)S(1)} %get-tuple-element.25), channel_id=1, source_target_pairs={{1,0},{2,1},{3,2},{5,4},{6,5},{7,6},{9,8},{10,9},{11,10},{13,12},{... | collective-permute-start | bytes 3145736 | tf_op jit(solution)/shard_map/ppermute | solution.py:14
  (22 other events, 85.5 us)
where the time goes:
time: 338 us; the launch traced here: 331 us
  matrix products  136 us (40%)
  waiting for transfers between devices  64.9 us (19%)
  starting transfers between devices  52.1 us (15%)
  local copies, waits for them, and re-layouts  49.6 us (15%)
  other arithmetic  26.9 us (8%)
    dot_general x36, matrix products, conv_local(): jnp.einsum('hwi,io->hwo', padded[row_off:row_off + row_count, col_off:col...  112 us
    ppermute x2, waiting for transfers between devices, from_behind(): return lax.ppermute(array, axis, pairs)  58.3 us
    ppermute x8, starting transfers between devices, padded_2(): lax.ppermute(lax.slice_in_dim(block, block.shape[dim] - width, None, axis...  27.5 us
    ppermute x8, starting transfers between devices, padded_2(): lax.ppermute(lax.slice_in_dim(block, 0, width, axis=dim), axis, backward)  19.1 us
    concatenate x7, other arithmetic, padded_2(): block = jnp.concatenate([low, block, high], axis=dim)  17 us
    slice x9, local copies, waits for them, and re-layouts, padded_2(): lax.slice_in_dim(block, block.shape[dim] - width, None, axis=dim)  12.2 us
    unnamed x109, local copies, waits for them, and re-layouts  10.6 us
    slice x5, local copies, waits for them, and re-layouts, padded_2(): lax.slice_in_dim(block, 0, width, axis=dim)  8.2 us
  transfers between devices with their start and end apart: 18, of which 5 were waited for; matrix products, arithmetic and copies ran while one was open for 19% of the time, Pallas kernels for 0%

commit v1 on v0

v1 whole, which is shorter than its diff:
```python
import functools
import math

import jax
import jax.numpy as jnp
from jax import lax
from jax.experimental import pallas as pl
from jax.experimental.pallas import tpu as pltpu
from jax.sharding import PartitionSpec as P

MESH = pl.DeviceIdType.MESH
F32 = jnp.float32
BF = jnp.bfloat16
BAND = 128
ROWS = 16
COLS = 256
WIDE = COLS + 16
HALO = 4
EXT = ROWS + 2 * HALO
CH = 128
CHUNK = 4
N_CHUNK = ROWS // CHUNK


def mm(a, b):
    return jnp.dot(a, b, preferred_element_type=F32)


def mm_nt(a, b):
    return lax.dot_general(a, b, (((1,), (1,)), ((), ())), preferred_element_type=F32)


def mm_tn(a, b):
    return lax.dot_general(a, b, (((0,), (0,)), ((), ())), preferred_element_type=F32)


def sig(v):
    return 0.5 * jnp.tanh(0.5 * v) + 0.5


def put3(ref, row, part, stride, val, forward):
    low = pltpu.roll(val, 1, 0)
    high = pltpu.roll(val, WIDE - 1, 0)
    order = (low, val, high) if forward else (high, val, low)
    for b in range(3):
        at = b * stride + part * CH
        ref[row, :, at : at + CH] = order[b].astype(BF)


def take(values, index):
    return jnp.take_along_axis(values, index, axis=1, mode="promise_in_bounds")


def kernel(
    n_rows, n_cols, taps, scale,
    fl_hbm, fr_hbm, hid_hbm, g_hbm, wg_hbm, wc_hbm, disp, mwp,
    nh, gl, gr,
    fl, fr, prev, far_out, far_in, near1, tap_near,
    hb, gb, mb, in3, ci3, cg3, upd, rst, mpre, cbm,
    wg, wc, wcp, wct, wgp, edge_lo, edge_hi,
    local, send, recv,
):
    rid = lax.axis_index("rows")
    cid = lax.axis_index("cols")
    radius = taps // 2

    has = {
        ("rows", -1): rid > 0,
        ("rows", 1): rid < n_rows - 1,
        ("cols", -1): cid > 0,
        ("cols", 1): cid < n_cols - 1,
    }

    def target(axis, step):
        return (rid + step, cid) if axis == "rows" else (rid, cid + step)

    def message(n, src, dst, axis, step):
        return pltpu.make_async_remote_copy(
            src_ref=src, dst_ref=dst, send_sem=send.at[n], recv_sem=recv.at[n],
            device_id=target(axis, step), device_id_type=MESH,
        )

    def start(spec):
        @pl.when(has[spec[3], spec[4]])
        def _():
            message(*spec).start()

    def finish_send(spec):
        @pl.when(has[spec[3], spec[4]])
        def _():
            message(*spec).wait_send()

    def finish_recv(spec):
        @pl.when(has[spec[3], -spec[4]])
        def _():
            message(*spec).wait_recv()

    own = pl.ds(HALO, ROWS)
    main = pl.ds(0, COLS)
    copies = [
        pltpu.make_async_copy(src, dst, local.at[n])
        for n, (src, dst) in enumerate(
            [
                (fl_hbm, fl),
                (fr_hbm, fr),
                (hid_hbm, hb.at[own, main]),
                (g_hbm, gb.at[own, main]),
                (wg_hbm, wg),
                (wc_hbm, wc),
            ]
        )
    ]
    for copy in copies:
        copy.start()

    barrier = pltpu.get_barrier_semaphore()
    for (axis, step), there in has.items():
        @pl.when(there)
        def _(axis=axis, step=step):
            pl.semaphore_signal(barrier, inc=1, device_id=target(axis, step), device_id_type=MESH)
    peers = sum(there.astype(jnp.int32) for there in has.values())
    pl.semaphore_wait(barrier, peers)

    last = pl.ds(COLS - 16, 16)
    first = pl.ds(0, 16)
    col_msgs = [
        (0, hid_hbm.at[:, last], edge_lo.at[0], "cols", 1),
        (1, hid_hbm.at[:, first], edge_hi.at[0], "cols", -1),
        (2, g_hbm.at[:, last], edge_lo.at[1], "cols", 1),
        (3, g_hbm.at[:, first], edge_hi.at[1], "cols", -1),
    ]
    block_msgs = [
        (
            4 + n,
            fr_hbm.at[pl.ds(n * CHUNK, CHUNK), pl.ds(COLS - BAND, BAND)],
            prev.at[pl.ds(n * CHUNK, CHUNK)],
            "cols",
            1,
        )
        for n in range(N_CHUNK)
    ]
    for spec in col_msgs + block_msgs:
        start(spec)

    def row_msgs(n, buf):
        return [
            (n, buf.at[pl.ds(HALO, HALO)], buf.at[pl.ds(HALO + ROWS, HALO)], "rows", -1),
            (n + 1, buf.at[pl.ds(ROWS, HALO)], buf.at[pl.ds(0, HALO)], "rows", 1),
        ]

    hid_rows, g_rows = row_msgs(8, hb), row_msgs(10, gb)
    motion_cols = [
        (12, mb.at[own, last], edge_lo.at[2], "cols", 1),
        (13, mb.at[own, first], edge_hi.at[2], "cols", -1),
    ]
    motion_rows = row_msgs(14, mb)
    far_msgs = [
        (
            16 + n,
            far_out.at[pl.ds(n * CHUNK, CHUNK)],
            far_in.at[pl.ds(n * CHUNK, CHUNK)],
            "cols",
            -1,
        )
        for n in range(N_CHUNK)
    ]

    @pl.when(jnp.logical_not(has["cols", -1]))
    def _():
        edge_lo[...] = jnp.zeros_like(edge_lo)
        prev[...] = jnp.zeros_like(prev)

    @pl.when(jnp.logical_not(has["cols", 1]))
    def _():
        edge_hi[...] = jnp.zeros_like(edge_hi)
        far_in[...] = jnp.zeros_like(far_in)

    @pl.when(jnp.logical_not(has["rows", -1]))
    def _():
        for buf in (hb, gb, mb):
            buf[0:HALO] = jnp.zeros((HALO, WIDE, CH), BF)

    @pl.when(jnp.logical_not(has["rows", 1]))
    def _():
        for buf in (hb, gb, mb):
            buf[HALO + ROWS : EXT] = jnp.zeros((HALO, WIDE, CH), BF)

    side = lax.broadcasted_iota(jnp.int32, (16, CH), 0) < 8

    def join_edges(which, buf):
        def one(r, carry):
            hi = edge_hi[which, r].astype(F32)
            lo = edge_lo[which, r].astype(F32)
            buf[HALO + r, COLS:WIDE, :] = jnp.where(side, hi, lo).astype(BF)
            return carry

        lax.fori_loop(0, ROWS, one, 0)

    for copy in copies:
        copy.wait()
    for spec in col_msgs:
        finish_recv(spec)
    join_edges(0, hb)
    join_edges(1, gb)
    for spec in hid_rows + g_rows:
        start(spec)

    wcp[...] = jnp.zeros_like(wcp)
    wgp[...] = jnp.zeros_like(wgp)
    for a in range(3):
        for b in range(3):
            t = a * 3 + b
            blk = wc[t * 256 : (t + 1) * 256, :]
            wcp[a * 768 + b * 256 : a * 768 + (b + 1) * 256, 0:CH] = blk
            wcp[(a + 1) * 768 + b * 256 : (a + 1) * 768 + (b + 1) * 256, CH : 2 * CH] = blk
            wct[t * CH : (t + 1) * CH, :] = blk.astype(F32).T.astype(BF)
            turned = wg[t * 256 + CH : (t + 1) * 256, :].astype(F32).T.astype(BF)
            q = 2 - a
            wgp[q * 768 + b * 256 : q * 768 + (b + 1) * 256, 0:CH] = turned
            wgp[(q + 1) * 768 + b * 256 : (q + 1) * 768 + (b + 1) * 256, CH : 2 * CH] = turned

    sub = lax.broadcasted_iota(jnp.int32, (BAND, BAND), 0)
    lane = lax.broadcasted_iota(jnp.int32, (BAND, BAND), 1)
    ones = jnp.ones((BAND, BAND), BF)

    def spread(r, b):
        line = disp[r, :, b * BAND : (b + 1) * BAND].astype(F32)
        diag = jnp.where(sub == lane, line, 0.0).astype(BF)
        return mm(diag, ones).astype(jnp.int32)

    def usable_of(levels0):
        level = levels0 + lane - radius
        return (level >= 0) & (level < BAND) & (lane < taps)

    def clip(v):
        return jnp.clip(v, 0, BAND - 1)

    def finish_motion(r, b, tap):
        pre = mm(tap.astype(BF), mwp[...])
        mpre[r, b * BAND : (b + 1) * BAND, :] = pre
        mb[HALO + r, b * BAND : (b + 1) * BAND, :] = (pre * sig(pre)).astype(BF)

    def near_row(r, carry):
        l0, l1 = fl[r, 0:BAND, :], fl[r, BAND:COLS, :]
        r0, r1 = fr[r, 0:BAND, :], fr[r, BAND:COLS, :]
        d0, d1 = spread(r, 0), spread(r, 1)
        c0 = sub + radius - d0 - lane
        tap_near[r] = jnp.where((c0 >= 0) & usable_of(d0), take(mm_nt(l0, r0) * scale, clip(c0)), 0.0)
        c1 = sub + radius - d1 - lane
        near = take(mm_nt(l1, r1) * scale, clip(c1))
        far = take(mm_nt(l1, r0) * scale, clip(c1 + BAND))
        finish_motion(r, 1, jnp.where(usable_of(d1), jnp.where(c1 >= 0, near, far), 0.0))
        return carry

    lax.fori_loop(0, ROWS, near_row, 0)

    for spec in hid_rows + g_rows:
        finish_recv(spec)

    def fill_hidden(r, carry):
        put3(in3, r, 0, 256, hb[r].astype(F32), True)
        return carry

    lax.fori_loop(0, EXT, fill_hidden, 0)

    def far_row(r, carry):
        d0 = spread(r, 0)
        c0 = sub + radius - d0 - lane
        far = take(mm_nt(fl[r, 0:BAND, :], prev[r]) * scale, clip(c0 + BAND))
        finish_motion(r, 0, jnp.where((c0 < 0) & usable_of(d0), far, tap_near[r]))
        return carry

    for n in range(N_CHUNK):
        finish_recv(block_msgs[n])
        lax.fori_loop(n * CHUNK, (n + 1) * CHUNK, far_row, 0)

    for spec in motion_cols:
        start(spec)
    for spec in motion_cols:
        finish_recv(spec)
    join_edges(2, mb)
    for spec in motion_rows:
        start(spec)

    def fill_motion(r, carry):
        m = mb[r].astype(F32)
        put3(in3, r, 1, 256, m, True)

        @pl.when((r >= 1) & (r < EXT - 1))
        def _():
            put3(ci3, r - 1, 1, 256, m, True)

        return carry

    def gate_row(r, carry):
        acc = mm(in3[r - 1], wg[0:768, :])
        acc = acc + mm(in3[r], wg[768:1536, :])
        acc = acc + mm(in3[r + 1], wg[1536:2304, :])
        reset = sig(acc[:, CH:])
        upd[r - 1] = sig(acc[:, :CH])
        rst[r - 1] = reset
        put3(ci3, r - 1, 0, 256, reset * hb[r].astype(F32), True)
        return carry

    lax.fori_loop(HALO, HALO + ROWS, fill_motion, 0)
    lax.fori_loop(HALO + 1, HALO + ROWS - 1, gate_row, 0)
    for spec in motion_rows:
        finish_recv(spec)
    lax.fori_loop(0, HALO, fill_motion, 0)
    lax.fori_loop(HALO + ROWS, EXT, fill_motion, 0)
    lax.fori_loop(1, HALO + 1, gate_row, 0)
    lax.fori_loop(HALO + ROWS - 1, EXT - 1, gate_row, 0)

    def cand_pair(r, inside):
        acc = mm(ci3[r - 2], wcp[0:768, :])
        for q in range(1, 4):
            acc = acc + mm(ci3[r - 2 + q], wcp[q * 768 : (q + 1) * 768, :])
        for s in range(2):
            c = jnp.tanh(acc[:, s * CH : (s + 1) * CH])
            u = upd[r + s - 1]
            h = hb[r + s].astype(F32)
            g = gb[r + s].astype(F32)
            if inside:
                nh[r + s - HALO] = ((1.0 - u) * h + u * c)[:COLS].astype(BF)
            put3(cg3, r + s - 2, 0, CH, g * u * (1.0 - c * c), False)
            put3(in3, r + s, 0, 256, g * (c - h) * u * (1.0 - u), False)

    def cand_inside(n, carry):
        cand_pair(HALO + 2 * n, True)
        return carry

    cand_pair(2, False)
    lax.fori_loop(0, ROWS // 2, cand_inside, 0)
    cand_pair(HALO + ROWS, False)

    def back_row(r, carry):
        acc = mm(cg3[r - 1], wct[0:384, :])
        acc = acc + mm(cg3[r - 2], wct[384:768, :])
        acc = acc + mm(cg3[r - 3], wct[768:1152, :])
        reset = rst[r - 1]
        grad = acc[:, :CH] * hb[r].astype(F32) * reset * (1.0 - reset)
        put3(in3, r, 1, 256, grad, False)
        cbm[r - 3] = acc[:, CH:]
        return carry

    lax.fori_loop(HALO - 1, HALO + ROWS + 1, back_row, 0)

    def tail_row(r, motion_grad):
        pre = mpre[r]
        s = sig(pre)
        pre_grad = (motion_grad * s * (1.0 + pre * (1.0 - s))).astype(BF)
        parts = []
        for b in range(2):
            d = spread(r, b)
            tap = mm_nt(pre_grad[b * BAND : (b + 1) * BAND, :], mwp[...])
            tap = jnp.where(usable_of(d), tap, 0.0)
            k = sub + radius - d - lane
            g_near = jnp.where(k >= 0, take(tap, clip(k)), 0.0).astype(BF)
            g_far = jnp.where(k + BAND >= 0, take(tap, clip(k + BAND)), 0.0).astype(BF)
            lb = fl[r, b * BAND : (b + 1) * BAND, :]
            rb = fr[r, b * BAND : (b + 1) * BAND, :]
            pb = prev[r] if b == 0 else fr[r, 0:BAND, :]
            gl[r, b * BAND : (b + 1) * BAND, :] = ((mm(g_near, rb) + mm(g_far, pb)) * scale).astype(BF)
            parts.append((mm_tn(g_near, lb) * scale, (mm_tn(g_far, lb) * scale).astype(BF)))
        far_out[r] = parts[0][1]
        gr[r, 0:BAND, :] = (parts[0][0] + parts[1][1].astype(F32)).astype(BF)
        near1[r] = parts[1][0]

    def tail_pair(n, carry):
        r = HALO + 2 * n
        acc = mm(in3[r - 1, 0:COLS], wgp[0:768, :])
        for q in range(1, 4):
            acc = acc + mm(in3[r - 1 + q, 0:COLS], wgp[q * 768 : (q + 1) * 768, :])
        for s in range(2):
            tail_row(2 * n + s, acc[:, s * CH : (s + 1) * CH] + cbm[r + s - 3, 0:COLS])
        return carry

    for n in range(N_CHUNK):
        lax.fori_loop(n * (CHUNK // 2), (n + 1) * (CHUNK // 2), tail_pair, 0)
        start(far_msgs[n])

    def add_far(r, carry):
        gr[r, BAND:COLS, :] = (near1[r] + far_in[r].astype(F32)).astype(BF)
        return carry

    for n in range(N_CHUNK):
        finish_recv(far_msgs[n])
        lax.fori_loop(n * CHUNK, (n + 1) * CHUNK, add_far, 0)
    for spec in col_msgs + block_msgs + hid_rows + g_rows + motion_cols + motion_rows + far_msgs:
        finish_send(spec)


def per_device(n_rows, n_cols, feat_left, feat_right, hidden, disparity, motion_weight, gate_weight, cand_weight, grad_hidden):
    taps = motion_weight.shape[0]
    feat = feat_left.shape[2]
    mwp = jnp.pad(motion_weight, ((0, BAND - taps), (0, 0)))
    wg = gate_weight.reshape(9 * 256, 256)
    wc = cand_weight.reshape(9 * 256, CH)
    hbm = pl.BlockSpec(memory_space=pl.ANY)
    vmem = pl.BlockSpec(memory_space=pltpu.VMEM)
    v = pltpu.VMEM
    return pl.pallas_call(
        functools.partial(kernel, n_rows, n_cols, taps, 1.0 / math.sqrt(feat)),
        out_shape=(
            jax.ShapeDtypeStruct(hidden.shape, BF),
            jax.ShapeDtypeStruct(feat_left.shape, BF),
            jax.ShapeDtypeStruct(feat_right.shape, BF),
        ),
        in_specs=[hbm] * 6 + [vmem] * 2,
        out_specs=(vmem,) * 3,
        scratch_shapes=[
            v((ROWS, COLS, feat), BF),
            v((ROWS, COLS, feat), BF),
            v((ROWS, BAND, feat), BF),
            v((ROWS, BAND, feat), BF),
            v((ROWS, BAND, feat), BF),
            v((ROWS, BAND, feat), F32),
            v((ROWS, BAND, BAND), F32),
            v((EXT, WIDE, CH), BF),
            v((EXT, WIDE, CH), BF),
            v((EXT, WIDE, CH), BF),
            v((EXT, WIDE, 6 * CH), BF),
            v((EXT - 2, WIDE, 6 * CH), BF),
            v((EXT - 4, WIDE, 3 * CH), BF),
            v((EXT - 2, WIDE, CH), F32),
            v((EXT - 2, WIDE, CH), F32),
            v((ROWS, COLS, CH), F32),
            v((ROWS + 2, WIDE, CH), F32),
            v((9 * 256, 256), BF),
            v((9 * 256, CH), BF),
            v((12 * 256, 256), BF),
            v((9 * CH, 256), BF),
            v((12 * 256, 256), BF),
            v((3, ROWS, 16, CH), BF),
            v((3, ROWS, 16, CH), BF),
            pltpu.SemaphoreType.DMA((6,)),
            pltpu.SemaphoreType.DMA((16 + N_CHUNK,)),
            pltpu.SemaphoreType.DMA((16 + N_CHUNK,)),
        ],
        compiler_params=pltpu.CompilerParams(
            collective_id=0, has_side_effects=True, vmem_limit_bytes=63 * 1024 * 1024
        ),
        cost_estimate=pl.CostEstimate(flops=17 * 10**9, bytes_accessed=14 * 10**6, transcendentals=0),
    )(feat_left, feat_right, hidden, grad_hidden, wg, wc, disparity[:, None, :], mwp)


def solution(mesh):
    blocks = P("rows", "cols", None)
    return jax.shard_map(
        functools.partial(per_device, mesh.shape["rows"], mesh.shape["cols"]),
        mesh=mesh,
        in_specs=(blocks, blocks, blocks, P("rows", "cols"), P(), P(), P(), blocks),
        out_specs=(blocks, blocks, blocks),
        check_vma=False,
    )
```

time: 338 us -> 106 us (0.31)
  the two profiles are of different devices: /device:TPU:11 before, /device:TPU:12 now
where the time goes in v1:
time: 106 us; the launch traced here: 104 us
  Pallas kernels  94.9 us (90%)
  local copies, waits for them, and re-layouts  8.76 us (8%)
    pallas_call x1, Pallas kernels, per_device(): pl.pallas_call(functools.partial(kernel, n_rows, n_cols, taps, 1.0 / math...  94.9 us
    unnamed x7, local copies, waits for them, and re-layouts  6.11 us

profile of v1, /device:TPU:12, one launch (start us, length us, event | category | flops | bytes accessed | tf_op | source)
XLA Modules:
  0.0 104.3 jit_solution(13197700240788505796)
XLA Ops:
  0.6 1.3 %broadcast_in_dim.3.disp = s32[16,1,256]{2,1,0:T(1,128)} reshape(s32[16,256]{1,0:T(8,128)} %param.11) | data formatting | bytes 32768 | tf_op jit(solution)/shard_map/broadcast_in_dim | solution.py:444
  2.0 1.3 %pad.4.mwp = bf16[128,128]{1,0:T(8,128)(2,1)} pad(bf16[9,128]{1,0:T(8,128)(2,1)} %param.12, bf16[]{:T(256)} %constant.2.clone.1), padding=0_119x0_0 | pad | bytes 35074 | tf_op jit(solution)/shard_map/jit(_pad)/pad | solution.py:396
  3.3 94.9 %shard_map.103 = (bf16[16,256,128]{2,1,0:T(8,128)(2,1)}, bf16[16,256,256]{2,1,0:T(8,128)(2,1)}, bf16[16,256,256]{2,1,0:T(8,128)(2,1)}) custom-call(bf16[16,256,256]{2,1,0:T(8,128)(2,1)} %fl_hbm.1, bf16[16,256,256]{2,1,0:T(8,128)(2,1)} %fr_hbm.1, bf16[16,256,128]{2,1,0:T(8,128)(2,1)} %hid_hbm.1, bf16[16,256,128]{2,1,0:T(8,128)(2,1)} %g_hbm.1, ...), custom_call_target="tpu_custom_call" | custom-call | flops 16999999488 | bytes 14000000 | tf_op jit(solution)/shard_map/pallas_call | solution.py:402
  98.2 0.0 copy-start.1
  98.2 2.4 %copy.14 = bf16[16,256,128]{2,1,0:T(8,128)(2,1)} copy(bf16[16,256,128]{2,1,0:T(8,128)(2,1)} %get-tuple-element.6) | data formatting | bytes 2097152
  100.7 0.0 copy-done.1
  100.7 0.0 copy-start
  100.7 1.3 %copy.15 = bf16[16,256,256]{2,1,0:T(8,128)(2,1)} copy(bf16[16,256,256]{2,1,0:T(8,128)(2,1)S(1)} %copy-done.1) | data formatting | bytes 4194304
  102.0 1.0 copy-done
  103.0 1.3 %copy.16 = bf16[16,256,256]{2,1,0:T(8,128)(2,1)} copy(bf16[16,256,256]{2,1,0:T(8,128)(2,1)S(1)} %copy-done) | data formatting | bytes 4194304
Async XLA Ops:
  98.2 2.5 %copy-start.1 = (bf16[16,256,256]{2,1,0:T(8,128)(2,1)S(1)}, bf16[16,256,256]{2,1,0:T(8,128)(2,1)}, u32[]{:S(2)}) copy-start(bf16[16,256,256]{2,1,0:T(8,128)(2,1)} %get-tuple-element.7) | copy-start | bytes 6291460
  100.7 2.3 %copy-start = (bf16[16,256,256]{2,1,0:T(8,128)(2,1)S(1)}, bf16[16,256,256]{2,1,0:T(8,128)(2,1)}, u32[]{:S(2)}) copy-start(bf16[16,256,256]{2,1,0:T(8,128)(2,1)} %get-tuple-element.8) | copy-start | bytes 6291460

commit v2 on v1

--- a/solution.py
+++ b/solution.py
@@ -18,8 +18,12 @@
 HALO = 4
 EXT = ROWS + 2 * HALO
 CH = 128
-CHUNK = 4
-N_CHUNK = ROWS // CHUNK
+FWD = 9
+BWD = ROWS - FWD
+TAP_PAD = 16
+FWD_CHUNKS = ((0, 3), (3, 3), (6, 3))
+BWD_CHUNKS = ((0, 4), (4, 3))
+N_MSG = 17 + 2 * len(FWD_CHUNKS) + 4 * len(BWD_CHUNKS)
 
 
 def mm(a, b):
@@ -53,9 +57,10 @@
 
 def kernel(
     n_rows, n_cols, taps, scale,
-    fl_hbm, fr_hbm, hid_hbm, g_hbm, wg_hbm, wc_hbm, disp, mwp,
+    fl_hbm, fr_hbm, hid_hbm, g_hbm, wg_hbm, wc_hbm, disp_in, mw,
     nh, gl, gr,
-    fl, fr, prev, far_out, far_in, near1, tap_near,
+    fl, fr, prev, left_in, disp_next, far_out, far_in, part_out, part_in, tap_out, tap_in,
+    near1, tap_near, disp, mwp,
     hb, gb, mb, in3, ci3, cg3, upd, rst, mpre, cbm,
     wg, wc, wcp, wct, wgp, edge_lo, edge_hi,
     local, send, recv,
@@ -129,18 +134,29 @@
         (2, g_hbm.at[:, last], edge_lo.at[1], "cols", 1),
         (3, g_hbm.at[:, first], edge_hi.at[1], "cols", -1),
     ]
-    block_msgs = [
-        (
-            4 + n,
-            fr_hbm.at[pl.ds(n * CHUNK, CHUNK), pl.ds(COLS - BAND, BAND)],
-            prev.at[pl.ds(n * CHUNK, CHUNK)],
-            "cols",
-            1,
-        )
-        for n in range(N_CHUNK)
-    ]
-    for spec in col_msgs + block_msgs:
+    bands = pl.ds(0, BAND)
+    tail_band = pl.ds(COLS - BAND, BAND)
+    base = 17
+    right_msgs, left_msgs, tap_msgs, slope_msgs, far_msgs, part_msgs = [], [], [], [], [], []
+    for at, size in FWD_CHUNKS:
+        rows = pl.ds(at, size)
+        right_msgs.append((base, fr_hbm.at[rows, tail_band], prev.at[rows], "cols", 1))
+        far_msgs.append((base + 1, far_out.at[rows], far_in.at[rows], "cols", -1))
+        base += 2
+    for at, size in BWD_CHUNKS:
+        rows, whole = pl.ds(at, size), pl.ds(FWD + at, size)
+        left_msgs.append((base, fl_hbm.at[whole, bands], left_in.at[rows], "cols", -1))
+        tap_msgs.append((base + 1, tap_out.at[0, rows], tap_in.at[0, rows], "cols", 1))
+        slope_msgs.append((base + 2, tap_out.at[1, rows], tap_in.at[1, rows], "cols", -1))
+        part_msgs.append((base + 3, part_out.at[rows], part_in.at[rows], "cols", 1))
+        base += 4
+    disp_msg = (16, disp.at[pl.ds(FWD, BWD)], disp_next, "cols", -1)
+    for r in range(ROWS):
+        disp[r] = disp_in[r : r + 1, :]
+    for spec in col_msgs + [disp_msg] + left_msgs + right_msgs:
         start(spec)
+    mwp[...] = jnp.zeros_like(mwp)
+    mwp[0:taps, :] = mw[...]
 
     def row_msgs(n, buf):
         return [
@@ -154,26 +170,20 @@
         (13, mb.at[own, first], edge_hi.at[2], "cols", -1),
     ]
     motion_rows = row_msgs(14, mb)
-    far_msgs = [
-        (
-            16 + n,
-            far_out.at[pl.ds(n * CHUNK, CHUNK)],
-            far_in.at[pl.ds(n * CHUNK, CHUNK)],
-            "cols",
-            -1,
-        )
-        for n in range(N_CHUNK)
-    ]
-
     @pl.when(jnp.logical_not(has["cols", -1]))
     def _():
         edge_lo[...] = jnp.zeros_like(edge_lo)
         prev[...] = jnp.zeros_like(prev)
+        tap_in[0] = jnp.zeros(tap_in.shape[1:], BF)
+        part_in[...] = jnp.zeros_like(part_in)
 
     @pl.when(jnp.logical_not(has["cols", 1]))
     def _():
         edge_hi[...] = jnp.zeros_like(edge_hi)
         far_in[...] = jnp.zeros_like(far_in)
+        left_in[...] = jnp.zeros_like(left_in)
+        disp_next[...] = jnp.zeros_like(disp_next)
+        tap_in[1] = jnp.zeros(tap_in.shape[1:], BF)
 
     @pl.when(jnp.logical_not(has["rows", -1]))
     def _():
@@ -223,10 +233,15 @@
     lane = lax.broadcasted_iota(jnp.int32, (BAND, BAND), 1)
     ones = jnp.ones((BAND, BAND), BF)
 
+    turn = (lax.broadcasted_iota(jnp.int32, (TAP_PAD, BAND), 0) == lax.broadcasted_iota(jnp.int32, (TAP_PAD, BAND), 1)).astype(BF)
+    back = (sub == lane).astype(BF)[0:TAP_PAD]
+
+    def spread_line(line):
+        diag = jnp.where(sub == lane, line.astype(F32), 0.0).astype(BF)
+        return mm(diag, ones).astype(jnp.int32)
+
     def spread(r, b):
-        line = disp[r, :, b * BAND : (b + 1) * BAND].astype(F32)
-        diag = jnp.where(sub == lane, line, 0.0).astype(BF)
-        return mm(diag, ones).astype(jnp.int32)
+        return spread_line(disp[r, :, b * BAND : (b + 1) * BAND])
 
     def usable_of(levels0):
         level = levels0 + lane - radius
@@ -235,8 +250,7 @@
     def clip(v):
         return jnp.clip(v, 0, BAND - 1)
 
-    def finish_motion(r, b, tap):
-        pre = mm(tap.astype(BF), mwp[...])
+    def finish_motion(r, b, pre):
         mpre[r, b * BAND : (b + 1) * BAND, :] = pre
         mb[HALO + r, b * BAND : (b + 1) * BAND, :] = (pre * sig(pre)).astype(BF)
 
@@ -249,10 +263,12 @@
         c1 = sub + radius - d1 - lane
         near = take(mm_nt(l1, r1) * scale, clip(c1))
         far = take(mm_nt(l1, r0) * scale, clip(c1 + BAND))
-        finish_motion(r, 1, jnp.where(usable_of(d1), jnp.where(c1 >= 0, near, far), 0.0))
+        tap = jnp.where(usable_of(d1), jnp.where(c1 >= 0, near, far), 0.0)
+        finish_motion(r, 1, mm(tap.astype(BF), mwp[...]))
         return carry
 
     lax.fori_loop(0, ROWS, near_row, 0)
+    start(motion_cols[0])
 
     for spec in hid_rows + g_rows:
         finish_recv(spec)
@@ -267,15 +283,41 @@
         d0 = spread(r, 0)
         c0 = sub + radius - d0 - lane
         far = take(mm_nt(fl[r, 0:BAND, :], prev[r]) * scale, clip(c0 + BAND))
-        finish_motion(r, 0, jnp.where((c0 < 0) & usable_of(d0), far, tap_near[r]))
-        return carry
-
-    for n in range(N_CHUNK):
-        finish_recv(block_msgs[n])
-        lax.fori_loop(n * CHUNK, (n + 1) * CHUNK, far_row, 0)
-
-    for spec in motion_cols:
-        start(spec)
+        tap = jnp.where((c0 < 0) & usable_of(d0), far, tap_near[r])
+        finish_motion(r, 0, mm(tap.astype(BF), mwp[...]))
+        return carry
+
+    def next_row(i, carry):
+        d = spread_line(disp_next[i, :, 0:BAND])
+        c = sub + radius - d - lane
+        far = take(mm_nt(left_in[i], fr[FWD + i, BAND:COLS, :]) * scale, clip(c + BAND))
+        tap = jnp.where((c < 0) & usable_of(d), far, 0.0).astype(BF)
+        tap_out[0, i] = mm_nt(turn, tap).astype(BF)
+        return carry
+
+    def taken_row(i, carry):
+        pre = mm(tap_near[FWD + i].astype(BF), mwp[...])
+        finish_motion(FWD + i, 0, pre + mm_tn(tap_in[0, i], mwp[0:TAP_PAD, :]))
+        return carry
+
+    def over(chunk, body):
+        lax.fori_loop(chunk[0], chunk[0] + chunk[1], body, 0)
+
+    finish_recv(disp_msg)
+    for n, chunk in enumerate(BWD_CHUNKS):
+        finish_recv(right_msgs[n])
+        over(FWD_CHUNKS[n], far_row)
+        finish_recv(left_msgs[n])
+        over(chunk, next_row)
+        start(tap_msgs[n])
+    for n in range(len(BWD_CHUNKS), len(FWD_CHUNKS)):
+        finish_recv(right_msgs[n])
+        over(FWD_CHUNKS[n], far_row)
+    for n, chunk in enumerate(BWD_CHUNKS):
+        finish_recv(tap_msgs[n])
+        over(chunk, taken_row)
+
+    start(motion_cols[1])
     for spec in motion_cols:
         finish_recv(spec)
     join_edges(2, mb)
@@ -345,55 +387,116 @@
 
     lax.fori_loop(HALO - 1, HALO + ROWS + 1, back_row, 0)
 
-    def tail_row(r, motion_grad):
-        pre = mpre[r]
-        s = sig(pre)
-        pre_grad = (motion_grad * s * (1.0 + pre * (1.0 - s))).astype(BF)
-        parts = []
-        for b in range(2):
-            d = spread(r, b)
-            tap = mm_nt(pre_grad[b * BAND : (b + 1) * BAND, :], mwp[...])
-            tap = jnp.where(usable_of(d), tap, 0.0)
-            k = sub + radius - d - lane
-            g_near = jnp.where(k >= 0, take(tap, clip(k)), 0.0).astype(BF)
-            g_far = jnp.where(k + BAND >= 0, take(tap, clip(k + BAND)), 0.0).astype(BF)
-            lb = fl[r, b * BAND : (b + 1) * BAND, :]
-            rb = fr[r, b * BAND : (b + 1) * BAND, :]
-            pb = prev[r] if b == 0 else fr[r, 0:BAND, :]
-            gl[r, b * BAND : (b + 1) * BAND, :] = ((mm(g_near, rb) + mm(g_far, pb)) * scale).astype(BF)
-            parts.append((mm_tn(g_near, lb) * scale, (mm_tn(g_far, lb) * scale).astype(BF)))
-        far_out[r] = parts[0][1]
-        gr[r, 0:BAND, :] = (parts[0][0] + parts[1][1].astype(F32)).astype(BF)
-        near1[r] = parts[1][0]
-
-    def tail_pair(n, carry):
-        r = HALO + 2 * n
-        acc = mm(in3[r - 1, 0:COLS], wgp[0:768, :])
-        for q in range(1, 4):
-            acc = acc + mm(in3[r - 1 + q, 0:COLS], wgp[q * 768 : (q + 1) * 768, :])
-        for s in range(2):
-            tail_row(2 * n + s, acc[:, s * CH : (s + 1) * CH] + cbm[r + s - 3, 0:COLS])
-        return carry
-
-    for n in range(N_CHUNK):
-        lax.fori_loop(n * (CHUNK // 2), (n + 1) * (CHUNK // 2), tail_pair, 0)
+    def slopes(n, b, store):
+        r = HALO + 4 * n
+        cut = slice(b * BAND, (b + 1) * BAND)
+        acc = None
+        for q in range(4):
+            lhs = jnp.concatenate([in3[r - 1 + q, cut], in3[r + 1 + q, cut]], axis=0)
+            term = mm(lhs, wgp[q * 768 : (q + 1) * 768, :])
+            acc = term if acc is None else acc + term
+        for s in range(4):
+            row = 4 * n + s
+            half = acc[(s // 2) * BAND : (s // 2 + 1) * BAND, (s % 2) * CH : (s % 2 + 1) * CH]
+            motion_grad = half + cbm[row + 1, cut]
+            pre = mpre[row, cut]
+            sg = sig(pre)
+            pre_grad = (motion_grad * sg * (1.0 + pre * (1.0 - sg))).astype(BF)
+            d = spread(row, b)
+            tap = jnp.where(usable_of(d), mm_nt(pre_grad, mwp[...]), 0.0)
+            store(row, d, tap)
+
+    def g_of(tap, d, shift):
+        k = sub + (radius + shift) - d - lane
+        return jnp.where(k >= 0, take(tap, clip(k)), 0.0).astype(BF)
+
+    def keep_tap(row, d, tap):
+        tap_near[row] = tap
+
+        @pl.when(row >= FWD)
+        def _():
+            tap_out[1, row - FWD] = mm_nt(turn, tap.astype(BF)).astype(BF)
+
+    def first_slopes(n, carry):
+        slopes(n, 0, keep_tap)
+        return carry
+
+    def send_far(r, carry):
+        g_far = g_of(tap_near[r], spread(r, 0), BAND)
+        far_out[r] = (mm_tn(g_far, fl[r, 0:BAND, :]) * scale).astype(BF)
+        return carry
+
+    def send_part(i, carry):
+        d = spread_line(disp_next[i, :, 0:BAND])
+        tap = mm_tn(tap_in[1, i], back)
+        g_far = g_of(tap, d, BAND)
+        part_out[i] = (mm(g_far, fr[FWD + i, BAND:COLS, :]) * scale).astype(BF)
+        near1[FWD + i] = mm_tn(g_far, left_in[i]) * scale
+        return carry
+
+    def own_second(row, d, tap):
+        g_near, g_far = g_of(tap, d, 0), g_of(tap, d, BAND)
+        l0, l1 = fl[row, 0:BAND, :], fl[row, BAND:COLS, :]
+        r0, r1 = fr[row, 0:BAND, :], fr[row, BAND:COLS, :]
+        gl[row, BAND:COLS, :] = ((mm(g_near, r1) + mm(g_far, r0)) * scale).astype(BF)
+        g_first = g_of(tap_near[row], spread(row, 0), 0)
+        far = (mm_tn(g_far, l1) * scale).astype(BF).astype(F32)
+        gr[row, 0:BAND, :] = (mm_tn(g_first, l0) * scale + far).astype(BF)
+        near = mm_tn(g_near, l1) * scale
+        first = mm(g_first, r0)
+
+        @pl.when(row < FWD)
+        def _():
+            g_back = g_of(tap_near[row], spread(row, 0), BAND)
+            gl[row, 0:BAND, :] = ((first + mm(g_back, prev[jnp.minimum(row, FWD - 1)])) * scale).astype(BF)
+            near1[row] = near
+
+        @pl.when(row >= FWD)
+        def _():
+            gr[row, BAND:COLS, :] = (near + near1[row].astype(BF).astype(F32)).astype(BF)
+            near1[row] = first * scale
+
+    def second_slopes(n, carry):
+        slopes(n, 1, own_second)
+        return carry
+
+    quads = ROWS // 4
+    split = FWD // 4
+    lax.fori_loop(split, quads, first_slopes, 0)
+    for spec in slope_msgs:
+        start(spec)
+    lax.fori_loop(0, split, first_slopes, 0)
+    for n, chunk in enumerate(FWD_CHUNKS):
+        over(chunk, send_far)
         start(far_msgs[n])
+    for n, chunk in enumerate(BWD_CHUNKS):
+        finish_recv(slope_msgs[n])
+        over(chunk, send_part)
+        start(part_msgs[n])
+    lax.fori_loop(0, quads, second_slopes, 0)
 
     def add_far(r, carry):
         gr[r, BAND:COLS, :] = (near1[r] + far_in[r].astype(F32)).astype(BF)
         return carry
 
-    for n in range(N_CHUNK):
+    def add_part(i, carry):
+        gl[FWD + i, 0:BAND, :] = (near1[FWD + i] + part_in[i].astype(F32)).astype(BF)
+        return carry
+
+    for n, chunk in enumerate(FWD_CHUNKS):
         finish_recv(far_msgs[n])
-        lax.fori_loop(n * CHUNK, (n + 1) * CHUNK, add_far, 0)
-    for spec in col_msgs + block_msgs + hid_rows + g_rows + motion_cols + motion_rows + far_msgs:
+        over(chunk, add_far)
+    for n, chunk in enumerate(BWD_CHUNKS):
+        finish_recv(part_msgs[n])
+        over(chunk, add_part)
+    sent = col_msgs + [disp_msg] + left_msgs + right_msgs + hid_rows + g_rows + motion_cols + motion_rows
+    for spec in sent + tap_msgs + slope_msgs + far_msgs + part_msgs:
         finish_send(spec)
 
 
 def per_device(n_rows, n_cols, feat_left, feat_right, hidden, disparity, motion_weight, gate_weight, cand_weight, grad_hidden):
     taps = motion_weight.shape[0]
     feat = feat_left.shape[2]
-    mwp = jnp.pad(motion_weight, ((0, BAND - taps), (0, 0)))
     wg = gate_weight.reshape(9 * 256, 256)
     wc = cand_weight.reshape(9 * 256, CH)
     hbm = pl.BlockSpec(memory_space=pl.ANY)
@@ -411,11 +514,19 @@
         scratch_shapes=[
             v((ROWS, COLS, feat), BF),
             v((ROWS, COLS, feat), BF),
-            v((ROWS, BAND, feat), BF),
-            v((ROWS, BAND, feat), BF),
-            v((ROWS, BAND, feat), BF),
+            v((FWD, BAND, feat), BF),
+            v((BWD, BAND, feat), BF),
+            v((BWD, 1, COLS), jnp.int32),
+            v((FWD, BAND, feat), BF),
+            v((FWD, BAND, feat), BF),
+            v((BWD, BAND, feat), BF),
+            v((BWD, BAND, feat), BF),
+            v((2, BWD, TAP_PAD, BAND), BF),
+            v((2, BWD, TAP_PAD, BAND), BF),
             v((ROWS, BAND, feat), F32),
             v((ROWS, BAND, BAND), F32),
+            v((ROWS, 1, COLS), jnp.int32),
+            v((BAND, CH), BF),
             v((EXT, WIDE, CH), BF),
             v((EXT, WIDE, CH), BF),
             v((EXT, WIDE, CH), BF),
@@ -434,14 +545,14 @@
             v((3, ROWS, 16, CH), BF),
             v((3, ROWS, 16, CH), BF),
             pltpu.SemaphoreType.DMA((6,)),
-            pltpu.SemaphoreType.DMA((16 + N_CHUNK,)),
-            pltpu.SemaphoreType.DMA((16 + N_CHUNK,)),
+            pltpu.SemaphoreType.DMA((N_MSG,)),
+            pltpu.SemaphoreType.DMA((N_MSG,)),
         ],
         compiler_params=pltpu.CompilerParams(
             collective_id=0, has_side_effects=True, vmem_limit_bytes=63 * 1024 * 1024
         ),
         cost_estimate=pl.CostEstimate(flops=17 * 10**9, bytes_accessed=14 * 10**6, transcendentals=0),
-    )(feat_left, feat_right, hidden, grad_hidden, wg, wc, disparity[:, None, :], mwp)
+    )(feat_left, feat_right, hidden, grad_hidden, wg, wc, disparity, motion_weight)
 
 
 def solution(mesh):

time: 106 us -> 103 us (0.972); the launches traced: 104 us -> 103 us
  local copies, waits for them, and re-layouts: 8.76 us -> 6.11 us
    broadcast_in_dim x1 -> x0, local copies, waits for them, and re-layouts: 1.33 us -> none  [per_device(): disparity[:, None, :]]
    pad x1 -> x0, local copies, waits for them, and re-layouts: 1.31 us -> none  [per_device(): mwp = jnp.pad(motion_weight, ((0, BAND - taps), (0, 0)))]
where the time goes in v2:
time: 103 us
  Pallas kernels  95.9 us (93%)
  local copies, waits for them, and re-layouts  6.11 us (6%)
    pallas_call x1, Pallas kernels, per_device(): pl.pallas_call(functools.partial(kernel, n_rows, n_cols, taps, 1.0 / math...  95.9 us
    unnamed x7, local copies, waits for them, and re-layouts  6.11 us

profile of v2, /device:TPU:12, one launch (start us, length us, event | category | flops | bytes accessed | tf_op | source)
XLA Modules:
  0.0 102.7 jit_solution(2574929424892513364)
XLA Ops:
  0.6 95.9 %shard_map.103 = (bf16[16,256,128]{2,1,0:T(8,128)(2,1)}, bf16[16,256,256]{2,1,0:T(8,128)(2,1)}, bf16[16,256,256]{2,1,0:T(8,128)(2,1)}) custom-call(bf16[16,256,256]{2,1,0:T(8,128)(2,1)} %fl_hbm.1, bf16[16,256,256]{2,1,0:T(8,128)(2,1)} %fr_hbm.1, bf16[16,256,128]{2,1,0:T(8,128)(2,1)} %hid_hbm.1, bf16[16,256,128]{2,1,0:T(8,128)(2,1)} %g_hbm.1, ...), custom_call_target="tpu_custom_call" | custom-call | flops 16999999488 | bytes 14000000 | tf_op jit(solution)/shard_map/pallas_call | solution.py:505
  96.6 0.0 copy-start.1
  96.6 2.4 %copy.14 = bf16[16,256,128]{2,1,0:T(8,128)(2,1)} copy(bf16[16,256,128]{2,1,0:T(8,128)(2,1)} %get-tuple-element.6) | data formatting | bytes 2097152
  99.0 0.0 copy-done.1
  99.0 0.0 copy-start
  99.0 1.3 %copy.15 = bf16[16,256,256]{2,1,0:T(8,128)(2,1)} copy(bf16[16,256,256]{2,1,0:T(8,128)(2,1)S(1)} %copy-done.1) | data formatting | bytes 4194304
  100.3 1.0 copy-done
  101.4 1.3 %copy.16 = bf16[16,256,256]{2,1,0:T(8,128)(2,1)} copy(bf16[16,256,256]{2,1,0:T(8,128)(2,1)S(1)} %copy-done) | data formatting | bytes 4194304
Async XLA Ops:
  96.6 2.5 %copy-start.1 = (bf16[16,256,256]{2,1,0:T(8,128)(2,1)S(1)}, bf16[16,256,256]{2,1,0:T(8,128)(2,1)}, u32[]{:S(2)}) copy-start(bf16[16,256,256]{2,1,0:T(8,128)(2,1)} %get-tuple-element.7) | copy-start | bytes 6291460
  99.0 2.3 %copy-start = (bf16[16,256,256]{2,1,0:T(8,128)(2,1)S(1)}, bf16[16,256,256]{2,1,0:T(8,128)(2,1)}, u32[]{:S(2)}) copy-start(bf16[16,256,256]{2,1,0:T(8,128)(2,1)} %get-tuple-element.8) | copy-start | bytes 6291460

commit v3 on v2

--- a/solution.py
+++ b/solution.py
@@ -49,6 +49,22 @@
     for b in range(3):
         at = b * stride + part * CH
         ref[row, :, at : at + CH] = order[b].astype(BF)
+
+
+def loop(low, high, body, by):
+    whole = (high - low) // by
+
+    def step(n, carry):
+        for s in range(by):
+            body(low + n * by + s)
+        return carry
+
+    if whole > 1:
+        lax.fori_loop(0, whole, step, 0)
+    elif whole == 1:
+        step(0, 0)
+    for n in range(low + whole * by, high):
+        body(n)
 
 
 def take(values, index):
@@ -198,15 +214,59 @@
     side = lax.broadcasted_iota(jnp.int32, (16, CH), 0) < 8
 
     def join_edges(which, buf):
-        def one(r, carry):
+        def one(r):
             hi = edge_hi[which, r].astype(F32)
             lo = edge_lo[which, r].astype(F32)
             buf[HALO + r, COLS:WIDE, :] = jnp.where(side, hi, lo).astype(BF)
-            return carry
-
-        lax.fori_loop(0, ROWS, one, 0)
-
-    for copy in copies:
+
+        loop(0, ROWS, one, 8)
+
+    sub = lax.broadcasted_iota(jnp.int32, (BAND, BAND), 0)
+    lane = lax.broadcasted_iota(jnp.int32, (BAND, BAND), 1)
+    ones = jnp.ones((BAND, BAND), BF)
+
+    turn = (lax.broadcasted_iota(jnp.int32, (TAP_PAD, BAND), 0) == lax.broadcasted_iota(jnp.int32, (TAP_PAD, BAND), 1)).astype(BF)
+    back = (sub == lane).astype(BF)[0:TAP_PAD]
+
+    def spread_line(line):
+        diag = jnp.where(sub == lane, line.astype(F32), 0.0).astype(BF)
+        return mm(diag, ones).astype(jnp.int32)
+
+    def spread(r, b):
+        return spread_line(disp[r, :, b * BAND : (b + 1) * BAND])
+
+    def usable_of(levels0):
+        level = levels0 + lane - radius
+        return (level >= 0) & (level < BAND) & (lane < taps)
+
+    def clip(v):
+        return jnp.clip(v, 0, BAND - 1)
+
+    def finish_motion(r, b, pre):
+        mpre[r, b * BAND : (b + 1) * BAND, :] = pre
+        mb[HALO + r, b * BAND : (b + 1) * BAND, :] = (pre * sig(pre)).astype(BF)
+
+    def near_row(n):
+        for s in range(4):
+            near_one(4 * n + s)
+
+    def near_one(r):
+        l0, l1 = fl[r, 0:BAND, :], fl[r, BAND:COLS, :]
+        r0, r1 = fr[r, 0:BAND, :], fr[r, BAND:COLS, :]
+        d0, d1 = spread(r, 0), spread(r, 1)
+        c0 = sub + radius - d0 - lane
+        tap_near[r] = jnp.where((c0 >= 0) & usable_of(d0), take(mm_nt(l0, r0) * scale, clip(c0)), 0.0)
+        c1 = sub + radius - d1 - lane
+        near = take(mm_nt(l1, r1) * scale, clip(c1))
+        far = take(mm_nt(l1, r0) * scale, clip(c1 + BAND))
+        tap = jnp.where(usable_of(d1), jnp.where(c1 >= 0, near, far), 0.0)
+        finish_motion(r, 1, mm(tap.astype(BF), mwp[...]))
+
+    for copy in copies[:2]:
+        copy.wait()
+    loop(0, ROWS // 4, near_row, 1)
+    start(motion_cols[0])
+    for copy in copies[2:4]:
         copy.wait()
     for spec in col_msgs:
         finish_recv(spec)
@@ -215,6 +275,8 @@
     for spec in hid_rows + g_rows:
         start(spec)
 
+    for copy in copies[4:]:
+        copy.wait()
     wcp[...] = jnp.zeros_like(wcp)
     wgp[...] = jnp.zeros_like(wgp)
     for a in range(3):
@@ -229,79 +291,35 @@
             wgp[q * 768 + b * 256 : q * 768 + (b + 1) * 256, 0:CH] = turned
             wgp[(q + 1) * 768 + b * 256 : (q + 1) * 768 + (b + 1) * 256, CH : 2 * CH] = turned
 
-    sub = lax.broadcasted_iota(jnp.int32, (BAND, BAND), 0)
-    lane = lax.broadcasted_iota(jnp.int32, (BAND, BAND), 1)
-    ones = jnp.ones((BAND, BAND), BF)
-
-    turn = (lax.broadcasted_iota(jnp.int32, (TAP_PAD, BAND), 0) == lax.broadcasted_iota(jnp.int32, (TAP_PAD, BAND), 1)).astype(BF)
-    back = (sub == lane).astype(BF)[0:TAP_PAD]
-
-    def spread_line(line):
-        diag = jnp.where(sub == lane, line.astype(F32), 0.0).astype(BF)
-        return mm(diag, ones).astype(jnp.int32)
-
-    def spread(r, b):
-        return spread_line(disp[r, :, b * BAND : (b + 1) * BAND])
-
-    def usable_of(levels0):
-        level = levels0 + lane - radius
-        return (level >= 0) & (level < BAND) & (lane < taps)
-
-    def clip(v):
-        return jnp.clip(v, 0, BAND - 1)
-
-    def finish_motion(r, b, pre):
-        mpre[r, b * BAND : (b + 1) * BAND, :] = pre
-        mb[HALO + r, b * BAND : (b + 1) * BAND, :] = (pre * sig(pre)).astype(BF)
-
-    def near_row(r, carry):
-        l0, l1 = fl[r, 0:BAND, :], fl[r, BAND:COLS, :]
-        r0, r1 = fr[r, 0:BAND, :], fr[r, BAND:COLS, :]
-        d0, d1 = spread(r, 0), spread(r, 1)
-        c0 = sub + radius - d0 - lane
-        tap_near[r] = jnp.where((c0 >= 0) & usable_of(d0), take(mm_nt(l0, r0) * scale, clip(c0)), 0.0)
-        c1 = sub + radius - d1 - lane
-        near = take(mm_nt(l1, r1) * scale, clip(c1))
-        far = take(mm_nt(l1, r0) * scale, clip(c1 + BAND))
-        tap = jnp.where(usable_of(d1), jnp.where(c1 >= 0, near, far), 0.0)
-        finish_motion(r, 1, mm(tap.astype(BF), mwp[...]))
-        return carry
-
-    lax.fori_loop(0, ROWS, near_row, 0)
-    start(motion_cols[0])
 
     for spec in hid_rows + g_rows:
         finish_recv(spec)
 
-    def fill_hidden(r, carry):
+    def fill_hidden(r):
         put3(in3, r, 0, 256, hb[r].astype(F32), True)
-        return carry
-
-    lax.fori_loop(0, EXT, fill_hidden, 0)
-
-    def far_row(r, carry):
+
+    loop(0, EXT, fill_hidden, 4)
+
+    def far_row(r):
         d0 = spread(r, 0)
         c0 = sub + radius - d0 - lane
         far = take(mm_nt(fl[r, 0:BAND, :], prev[r]) * scale, clip(c0 + BAND))
         tap = jnp.where((c0 < 0) & usable_of(d0), far, tap_near[r])
         finish_motion(r, 0, mm(tap.astype(BF), mwp[...]))
-        return carry
-
-    def next_row(i, carry):
+
+    def next_row(i):
         d = spread_line(disp_next[i, :, 0:BAND])
         c = sub + radius - d - lane
         far = take(mm_nt(left_in[i], fr[FWD + i, BAND:COLS, :]) * scale, clip(c + BAND))
         tap = jnp.where((c < 0) & usable_of(d), far, 0.0).astype(BF)
         tap_out[0, i] = mm_nt(turn, tap).astype(BF)
-        return carry
-
-    def taken_row(i, carry):
+
+    def taken_row(i):
         pre = mm(tap_near[FWD + i].astype(BF), mwp[...])
         finish_motion(FWD + i, 0, pre + mm_tn(tap_in[0, i], mwp[0:TAP_PAD, :]))
-        return carry
 
     def over(chunk, body):
-        lax.fori_loop(chunk[0], chunk[0] + chunk[1], body, 0)
+        loop(chunk[0], chunk[0] + chunk[1], body, chunk[1])
 
     finish_recv(disp_msg)
     for n, chunk in enumerate(BWD_CHUNKS):
@@ -324,68 +342,71 @@
     for spec in motion_rows:
         start(spec)
 
-    def fill_motion(r, carry):
+    def fill_motion(r):
         m = mb[r].astype(F32)
         put3(in3, r, 1, 256, m, True)
-
-        @pl.when((r >= 1) & (r < EXT - 1))
-        def _():
-            put3(ci3, r - 1, 1, 256, m, True)
-
-        return carry
-
-    def gate_row(r, carry):
-        acc = mm(in3[r - 1], wg[0:768, :])
-        acc = acc + mm(in3[r], wg[768:1536, :])
-        acc = acc + mm(in3[r + 1], wg[1536:2304, :])
-        reset = sig(acc[:, CH:])
-        upd[r - 1] = sig(acc[:, :CH])
-        rst[r - 1] = reset
-        put3(ci3, r - 1, 0, 256, reset * hb[r].astype(F32), True)
-        return carry
-
-    lax.fori_loop(HALO, HALO + ROWS, fill_motion, 0)
-    lax.fori_loop(HALO + 1, HALO + ROWS - 1, gate_row, 0)
+        put3(ci3, r - 1, 1, 256, m, True)
+
+    def rows_of(ref, r, count):
+        return ref[pl.ds(r, count)].reshape(count * WIDE, ref.shape[2])
+
+    def gate_pair(r):
+        acc = mm(rows_of(in3, r - 1, 2), wg[0:768, :])
+        acc = acc + mm(rows_of(in3, r, 2), wg[768:1536, :])
+        acc = acc + mm(rows_of(in3, r + 1, 2), wg[1536:2304, :])
+        for s in range(2):
+            part = acc[s * WIDE : (s + 1) * WIDE]
+            reset = sig(part[:, CH:])
+            upd[r + s - 1] = sig(part[:, :CH])
+            rst[r + s - 1] = reset
+            put3(ci3, r + s - 1, 0, 256, reset * hb[r + s].astype(F32), True)
+
+    loop(HALO, HALO + ROWS, fill_motion, 4)
+    loop(0, ROWS // 2 - 1, lambda n: gate_pair(HALO + 1 + 2 * n), 2)
     for spec in motion_rows:
         finish_recv(spec)
-    lax.fori_loop(0, HALO, fill_motion, 0)
-    lax.fori_loop(HALO + ROWS, EXT, fill_motion, 0)
-    lax.fori_loop(1, HALO + 1, gate_row, 0)
-    lax.fori_loop(HALO + ROWS - 1, EXT - 1, gate_row, 0)
-
-    def cand_pair(r, inside):
-        acc = mm(ci3[r - 2], wcp[0:768, :])
-        for q in range(1, 4):
-            acc = acc + mm(ci3[r - 2 + q], wcp[q * 768 : (q + 1) * 768, :])
-        for s in range(2):
-            c = jnp.tanh(acc[:, s * CH : (s + 1) * CH])
+    mb_top = EXT - 1
+    loop(1, HALO, fill_motion, HALO - 1)
+    loop(HALO + ROWS, mb_top, fill_motion, HALO - 1)
+    put3(in3, 0, 1, 256, mb[0].astype(F32), True)
+    put3(in3, mb_top, 1, 256, mb[mb_top].astype(F32), True)
+    loop(0, 2, lambda n: gate_pair(1 + 2 * n), 2)
+    loop(0, 2, lambda n: gate_pair(HALO + ROWS - 1 + 2 * n), 2)
+
+    def cand_quad(n, kept):
+        r = 2 + 4 * n
+        acc = None
+        for q in range(4):
+            lhs = jnp.concatenate([ci3[r - 2 + q], ci3[r + q]], axis=0)
+            term = mm(lhs, wcp[q * 768 : (q + 1) * 768, :])
+            acc = term if acc is None else acc + term
+        for s in range(4):
+            c = jnp.tanh(acc[(s // 2) * WIDE : (s // 2 + 1) * WIDE, (s % 2) * CH : (s % 2 + 1) * CH])
             u = upd[r + s - 1]
             h = hb[r + s].astype(F32)
             g = gb[r + s].astype(F32)
-            if inside:
+            if kept[s]:
                 nh[r + s - HALO] = ((1.0 - u) * h + u * c)[:COLS].astype(BF)
             put3(cg3, r + s - 2, 0, CH, g * u * (1.0 - c * c), False)
             put3(in3, r + s, 0, 256, g * (c - h) * u * (1.0 - u), False)
 
-    def cand_inside(n, carry):
-        cand_pair(HALO + 2 * n, True)
-        return carry
-
-    cand_pair(2, False)
-    lax.fori_loop(0, ROWS // 2, cand_inside, 0)
-    cand_pair(HALO + ROWS, False)
-
-    def back_row(r, carry):
-        acc = mm(cg3[r - 1], wct[0:384, :])
-        acc = acc + mm(cg3[r - 2], wct[384:768, :])
-        acc = acc + mm(cg3[r - 3], wct[768:1152, :])
-        reset = rst[r - 1]
-        grad = acc[:, :CH] * hb[r].astype(F32) * reset * (1.0 - reset)
-        put3(in3, r, 1, 256, grad, False)
-        cbm[r - 3] = acc[:, CH:]
-        return carry
-
-    lax.fori_loop(HALO - 1, HALO + ROWS + 1, back_row, 0)
+    cand_quad(0, (False, False, True, True))
+    loop(1, 4, lambda n: cand_quad(n, (True,) * 4), 1)
+    cand_quad(4, (True, True, False, False))
+
+    def back_pair(n):
+        r = HALO - 1 + 2 * n
+        acc = mm(rows_of(cg3, r - 1, 2), wct[0:384, :])
+        acc = acc + mm(rows_of(cg3, r - 2, 2), wct[384:768, :])
+        acc = acc + mm(rows_of(cg3, r - 3, 2), wct[768:1152, :])
+        for s in range(2):
+            part = acc[s * WIDE : (s + 1) * WIDE]
+            reset = rst[r + s - 1]
+            grad = part[:, :CH] * hb[r + s].astype(F32) * reset * (1.0 - reset)
+            put3(in3, r + s, 1, 256, grad, False)
+            cbm[r + s - 3] = part[:, CH:]
+
+    loop(0, ROWS // 2 + 1, back_pair, 3)
 
     def slopes(n, b, store):
         r = HALO + 4 * n
@@ -412,27 +433,19 @@
 
     def keep_tap(row, d, tap):
         tap_near[row] = tap
-
-        @pl.when(row >= FWD)
-        def _():
+        if row >= FWD:
             tap_out[1, row - FWD] = mm_nt(turn, tap.astype(BF)).astype(BF)
 
-    def first_slopes(n, carry):
-        slopes(n, 0, keep_tap)
-        return carry
-
-    def send_far(r, carry):
+    def send_far(r):
         g_far = g_of(tap_near[r], spread(r, 0), BAND)
         far_out[r] = (mm_tn(g_far, fl[r, 0:BAND, :]) * scale).astype(BF)
-        return carry
-
-    def send_part(i, carry):
+
+    def send_part(i):
         d = spread_line(disp_next[i, :, 0:BAND])
         tap = mm_tn(tap_in[1, i], back)
         g_far = g_of(tap, d, BAND)
         part_out[i] = (mm(g_far, fr[FWD + i, BAND:COLS, :]) * scale).astype(BF)
         near1[FWD + i] = mm_tn(g_far, left_in[i]) * scale
-        return carry
 
     def own_second(row, d, tap):
         g_near, g_far = g_of(tap, d, 0), g_of(tap, d, BAND)
@@ -445,27 +458,22 @@
         near = mm_tn(g_near, l1) * scale
         first = mm(g_first, r0)
 
-        @pl.when(row < FWD)
-        def _():
+        if row < FWD:
             g_back = g_of(tap_near[row], spread(row, 0), BAND)
-            gl[row, 0:BAND, :] = ((first + mm(g_back, prev[jnp.minimum(row, FWD - 1)])) * scale).astype(BF)
+            gl[row, 0:BAND, :] = ((first + mm(g_back, prev[row])) * scale).astype(BF)
             near1[row] = near
-
-        @pl.when(row >= FWD)
-        def _():
+        else:
             gr[row, BAND:COLS, :] = (near + near1[row].astype(BF).astype(F32)).astype(BF)
             near1[row] = first * scale
 
-    def second_slopes(n, carry):
-        slopes(n, 1, own_second)
-        return carry
-
     quads = ROWS // 4
     split = FWD // 4
-    lax.fori_loop(split, quads, first_slopes, 0)
+    for n in range(split, quads):
+        slopes(n, 0, keep_tap)
     for spec in slope_msgs:
         start(spec)
-    lax.fori_loop(0, split, first_slopes, 0)
+    for n in range(split):
+        slopes(n, 0, keep_tap)
     for n, chunk in enumerate(FWD_CHUNKS):
         over(chunk, send_far)
         start(far_msgs[n])
@@ -473,15 +481,14 @@
         finish_recv(slope_msgs[n])
         over(chunk, send_part)
         start(part_msgs[n])
-    lax.fori_loop(0, quads, second_slopes, 0)
-
-    def add_far(r, carry):
+    for n in range(quads):
+        slopes(n, 1, own_second)
+
+    def add_far(r):
         gr[r, BAND:COLS, :] = (near1[r] + far_in[r].astype(F32)).astype(BF)
-        return carry
-
-    def add_part(i, carry):
+
+    def add_part(i):
         gl[FWD + i, 0:BAND, :] = (near1[FWD + i] + part_in[i].astype(F32)).astype(BF)
-        return carry
 
     for n, chunk in enumerate(FWD_CHUNKS):
         finish_recv(far_msgs[n])

time: 103 us -> 91.2 us (0.89)
  Pallas kernels: 95.9 us -> 84.2 us
    pallas_call x1, Pallas kernels: 95.9 us -> 84.2 us  [per_device(): pl.pallas_call(functools.partial(kernel, n_rows, n_cols, taps, 1.0 / math...]
where the time goes in v3:
time: 91.2 us; the launch traced here: 90.9 us
  Pallas kernels  84.2 us (92%)
  local copies, waits for them, and re-layouts  6.11 us (7%)
    pallas_call x1, Pallas kernels, per_device(): pl.pallas_call(functools.partial(kernel, n_rows, n_cols, taps, 1.0 / math...  84.2 us
    unnamed x7, local copies, waits for them, and re-layouts  6.11 us

profile of v3, /device:TPU:12, one launch (start us, length us, event | category | flops | bytes accessed | tf_op | source)
XLA Modules:
  0.0 90.9 jit_solution(6034007061936194035)
XLA Ops:
  0.6 84.2 %shard_map.103 = (bf16[16,256,128]{2,1,0:T(8,128)(2,1)}, bf16[16,256,256]{2,1,0:T(8,128)(2,1)}, bf16[16,256,256]{2,1,0:T(8,128)(2,1)}) custom-call(bf16[16,256,256]{2,1,0:T(8,128)(2,1)} %fl_hbm.1, bf16[16,256,256]{2,1,0:T(8,128)(2,1)} %fr_hbm.1, bf16[16,256,128]{2,1,0:T(8,128)(2,1)} %hid_hbm.1, bf16[16,256,128]{2,1,0:T(8,128)(2,1)} %g_hbm.1, ...), custom_call_target="tpu_custom_call" | custom-call | flops 16999999488 | bytes 14000000 | tf_op jit(solution)/shard_map/pallas_call | solution.py:512
  84.8 0.0 copy-start.1
  84.8 2.4 %copy.14 = bf16[16,256,128]{2,1,0:T(8,128)(2,1)} copy(bf16[16,256,128]{2,1,0:T(8,128)(2,1)} %get-tuple-element.6) | data formatting | bytes 2097152
  87.3 0.0 copy-done.1
  87.3 0.0 copy-start
  87.3 1.3 %copy.15 = bf16[16,256,256]{2,1,0:T(8,128)(2,1)} copy(bf16[16,256,256]{2,1,0:T(8,128)(2,1)S(1)} %copy-done.1) | data formatting | bytes 4194304
  88.6 1.0 %copy-done = bf16[16,256,256]{2,1,0:T(8,128)(2,1)S(1)} copy-done((bf16[16,256,256]{2,1,0:T(8,128)(2,1)S(1)}, bf16[16,256,256]{2,1,0:T(8,128)(2,1)}, u32[]{:S(2)}) %copy-start) | copy-done | bytes 2097176
  89.6 1.3 %copy.16 = bf16[16,256,256]{2,1,0:T(8,128)(2,1)} copy(bf16[16,256,256]{2,1,0:T(8,128)(2,1)S(1)} %copy-done) | data formatting | bytes 4194304
Async XLA Ops:
  84.8 2.5 %copy-start.1 = (bf16[16,256,256]{2,1,0:T(8,128)(2,1)S(1)}, bf16[16,256,256]{2,1,0:T(8,128)(2,1)}, u32[]{:S(2)}) copy-start(bf16[16,256,256]{2,1,0:T(8,128)(2,1)} %get-tuple-element.7) | copy-start | bytes 6291460
  87.3 2.3 %copy-start = (bf16[16,256,256]{2,1,0:T(8,128)(2,1)S(1)}, bf16[16,256,256]{2,1,0:T(8,128)(2,1)}, u32[]{:S(2)}) copy-start(bf16[16,256,256]{2,1,0:T(8,128)(2,1)} %get-tuple-element.8) | copy-start | bytes 6291460

commit v4 on v3

--- a/solution.py
+++ b/solution.py
@@ -42,13 +42,15 @@
     return 0.5 * jnp.tanh(0.5 * v) + 0.5
 
 
-def put3(ref, row, part, stride, val, forward):
+def put3(places, part, stride, val, forward):
     low = pltpu.roll(val, 1, 0)
     high = pltpu.roll(val, WIDE - 1, 0)
     order = (low, val, high) if forward else (high, val, low)
     for b in range(3):
         at = b * stride + part * CH
-        ref[row, :, at : at + CH] = order[b].astype(BF)
+        kept = order[b].astype(BF)
+        for ref, row in places:
+            ref[row, :, at : at + CH] = kept
 
 
 def loop(low, high, body, by):
@@ -76,7 +78,7 @@
     fl_hbm, fr_hbm, hid_hbm, g_hbm, wg_hbm, wc_hbm, disp_in, mw,
     nh, gl, gr,
     fl, fr, prev, left_in, disp_next, far_out, far_in, part_out, part_in, tap_out, tap_in,
-    near1, tap_near, disp, mwp,
+    near1, tap_near, cols, disp, mwp,
     hb, gb, mb, in3, ci3, cg3, upd, rst, mpre, cbm,
     wg, wc, wcp, wct, wgp, edge_lo, edge_hi,
     local, send, recv,
@@ -232,15 +234,18 @@
         diag = jnp.where(sub == lane, line.astype(F32), 0.0).astype(BF)
         return mm(diag, ones).astype(jnp.int32)
 
-    def spread(r, b):
-        return spread_line(disp[r, :, b * BAND : (b + 1) * BAND])
-
-    def usable_of(levels0):
-        level = levels0 + lane - radius
+    def column_of(line):
+        return sub + radius - spread_line(line) - lane
+
+    def usable_of(col):
+        level = sub - col
         return (level >= 0) & (level < BAND) & (lane < taps)
 
-    def clip(v):
-        return jnp.clip(v, 0, BAND - 1)
+    def pick(values, col):
+        return take(values, col & (BAND - 1))
+
+    def g_of(picked, col, shift):
+        return jnp.where(((col + shift) & -TAP_PAD) == 0, picked, 0.0).astype(BF)
 
     def finish_motion(r, b, pre):
         mpre[r, b * BAND : (b + 1) * BAND, :] = pre
@@ -251,15 +256,15 @@
             near_one(4 * n + s)
 
     def near_one(r):
-        l0, l1 = fl[r, 0:BAND, :], fl[r, BAND:COLS, :]
-        r0, r1 = fr[r, 0:BAND, :], fr[r, BAND:COLS, :]
-        d0, d1 = spread(r, 0), spread(r, 1)
-        c0 = sub + radius - d0 - lane
-        tap_near[r] = jnp.where((c0 >= 0) & usable_of(d0), take(mm_nt(l0, r0) * scale, clip(c0)), 0.0)
-        c1 = sub + radius - d1 - lane
-        near = take(mm_nt(l1, r1) * scale, clip(c1))
-        far = take(mm_nt(l1, r0) * scale, clip(c1 + BAND))
-        tap = jnp.where(usable_of(d1), jnp.where(c1 >= 0, near, far), 0.0)
+        c0 = column_of(disp[r, :, 0:BAND])
+        c1 = column_of(disp[r, :, BAND:COLS])
+        cols[0, r] = c0
+        cols[1, r] = c1
+        near = pick(mm_nt(fl[r, 0:BAND, :], fr[r, 0:BAND, :]), c0)
+        tap_near[r] = jnp.where((c0 >= 0) & usable_of(c0), near, 0.0) * scale
+        both = mm_nt(fl[r, BAND:COLS, :], fr[r])
+        tap = jnp.where(c1 >= 0, pick(both[:, BAND:], c1), pick(both[:, :BAND], c1))
+        tap = jnp.where(usable_of(c1), tap, 0.0) * scale
         finish_motion(r, 1, mm(tap.astype(BF), mwp[...]))
 
     for copy in copies[:2]:
@@ -296,22 +301,20 @@
         finish_recv(spec)
 
     def fill_hidden(r):
-        put3(in3, r, 0, 256, hb[r].astype(F32), True)
+        put3(((in3, r),), 0, 256, hb[r].astype(F32), True)
 
     loop(0, EXT, fill_hidden, 4)
 
     def far_row(r):
-        d0 = spread(r, 0)
-        c0 = sub + radius - d0 - lane
-        far = take(mm_nt(fl[r, 0:BAND, :], prev[r]) * scale, clip(c0 + BAND))
-        tap = jnp.where((c0 < 0) & usable_of(d0), far, tap_near[r])
+        c0 = cols[0, r]
+        far = pick(mm_nt(fl[r, 0:BAND, :], prev[r]), c0) * scale
+        tap = jnp.where((c0 < 0) & usable_of(c0), far, tap_near[r])
         finish_motion(r, 0, mm(tap.astype(BF), mwp[...]))
 
     def next_row(i):
-        d = spread_line(disp_next[i, :, 0:BAND])
-        c = sub + radius - d - lane
-        far = take(mm_nt(left_in[i], fr[FWD + i, BAND:COLS, :]) * scale, clip(c + BAND))
-        tap = jnp.where((c < 0) & usable_of(d), far, 0.0).astype(BF)
+        c = column_of(disp_next[i, :, 0:BAND])
+        far = pick(mm_nt(left_in[i], fr[FWD + i, BAND:COLS, :]), c) * scale
+        tap = jnp.where((c < 0) & usable_of(c), far, 0.0).astype(BF)
         tap_out[0, i] = mm_nt(turn, tap).astype(BF)
 
     def taken_row(i):
@@ -344,8 +347,7 @@
 
     def fill_motion(r):
         m = mb[r].astype(F32)
-        put3(in3, r, 1, 256, m, True)
-        put3(ci3, r - 1, 1, 256, m, True)
+        put3(((in3, r), (ci3, r - 1)), 1, 256, m, True)
 
     def rows_of(ref, r, count):
         return ref[pl.ds(r, count)].reshape(count * WIDE, ref.shape[2])
@@ -359,7 +361,7 @@
             reset = sig(part[:, CH:])
             upd[r + s - 1] = sig(part[:, :CH])
             rst[r + s - 1] = reset
-            put3(ci3, r + s - 1, 0, 256, reset * hb[r + s].astype(F32), True)
+            put3(((ci3, r + s - 1),), 0, 256, reset * hb[r + s].astype(F32), True)
 
     loop(HALO, HALO + ROWS, fill_motion, 4)
     loop(0, ROWS // 2 - 1, lambda n: gate_pair(HALO + 1 + 2 * n), 2)
@@ -368,8 +370,8 @@
     mb_top = EXT - 1
     loop(1, HALO, fill_motion, HALO - 1)
     loop(HALO + ROWS, mb_top, fill_motion, HALO - 1)
-    put3(in3, 0, 1, 256, mb[0].astype(F32), True)
-    put3(in3, mb_top, 1, 256, mb[mb_top].astype(F32), True)
+    put3(((in3, 0),), 1, 256, mb[0].astype(F32), True)
+    put3(((in3, mb_top),), 1, 256, mb[mb_top].astype(F32), True)
     loop(0, 2, lambda n: gate_pair(1 + 2 * n), 2)
     loop(0, 2, lambda n: gate_pair(HALO + ROWS - 1 + 2 * n), 2)
 
@@ -387,8 +389,8 @@
             g = gb[r + s].astype(F32)
             if kept[s]:
                 nh[r + s - HALO] = ((1.0 - u) * h + u * c)[:COLS].astype(BF)
-            put3(cg3, r + s - 2, 0, CH, g * u * (1.0 - c * c), False)
-            put3(in3, r + s, 0, 256, g * (c - h) * u * (1.0 - u), False)
+            put3(((cg3, r + s - 2),), 0, CH, g * u * (1.0 - c * c), False)
+            put3(((in3, r + s),), 0, 256, g * (c - h) * u * (1.0 - u), False)
 
     cand_quad(0, (False, False, True, True))
     loop(1, 4, lambda n: cand_quad(n, (True,) * 4), 1)
@@ -403,7 +405,7 @@
             part = acc[s * WIDE : (s + 1) * WIDE]
             reset = rst[r + s - 1]
             grad = part[:, :CH] * hb[r + s].astype(F32) * reset * (1.0 - reset)
-            put3(in3, r + s, 1, 256, grad, False)
+            put3(((in3, r + s),), 1, 256, grad, False)
             cbm[r + s - 3] = part[:, CH:]
 
     loop(0, ROWS // 2 + 1, back_pair, 3)
@@ -423,43 +425,39 @@
             pre = mpre[row, cut]
             sg = sig(pre)
             pre_grad = (motion_grad * sg * (1.0 + pre * (1.0 - sg))).astype(BF)
-            d = spread(row, b)
-            tap = jnp.where(usable_of(d), mm_nt(pre_grad, mwp[...]), 0.0)
-            store(row, d, tap)
-
-    def g_of(tap, d, shift):
-        k = sub + (radius + shift) - d - lane
-        return jnp.where(k >= 0, take(tap, clip(k)), 0.0).astype(BF)
-
-    def keep_tap(row, d, tap):
-        tap_near[row] = tap
+            col = cols[b, row]
+            tap = jnp.where(usable_of(col), mm_nt(pre_grad, mwp[...]), 0.0)
+            store(row, col, tap)
+
+    def keep_tap(row, col, tap):
+        tap_near[row] = pick(tap, col)
         if row >= FWD:
             tap_out[1, row - FWD] = mm_nt(turn, tap.astype(BF)).astype(BF)
 
     def send_far(r):
-        g_far = g_of(tap_near[r], spread(r, 0), BAND)
+        g_far = g_of(tap_near[r], cols[0, r], BAND)
         far_out[r] = (mm_tn(g_far, fl[r, 0:BAND, :]) * scale).astype(BF)
 
     def send_part(i):
-        d = spread_line(disp_next[i, :, 0:BAND])
-        tap = mm_tn(tap_in[1, i], back)
-        g_far = g_of(tap, d, BAND)
+        col = column_of(disp_next[i, :, 0:BAND])
+        g_far = g_of(pick(mm_tn(tap_in[1, i], back), col), col, BAND)
         part_out[i] = (mm(g_far, fr[FWD + i, BAND:COLS, :]) * scale).astype(BF)
         near1[FWD + i] = mm_tn(g_far, left_in[i]) * scale
 
-    def own_second(row, d, tap):
-        g_near, g_far = g_of(tap, d, 0), g_of(tap, d, BAND)
-        l0, l1 = fl[row, 0:BAND, :], fl[row, BAND:COLS, :]
-        r0, r1 = fr[row, 0:BAND, :], fr[row, BAND:COLS, :]
-        gl[row, BAND:COLS, :] = ((mm(g_near, r1) + mm(g_far, r0)) * scale).astype(BF)
-        g_first = g_of(tap_near[row], spread(row, 0), 0)
-        far = (mm_tn(g_far, l1) * scale).astype(BF).astype(F32)
-        gr[row, 0:BAND, :] = (mm_tn(g_first, l0) * scale + far).astype(BF)
-        near = mm_tn(g_near, l1) * scale
-        first = mm(g_first, r0)
+    def own_second(row, col, tap):
+        picked = pick(tap, col)
+        g_both = jnp.concatenate([g_of(picked, col, BAND), g_of(picked, col, 0)], axis=1)
+        gl[row, BAND:COLS, :] = (mm(g_both, fr[row]) * scale).astype(BF)
+        grads = mm_tn(g_both, fl[row, BAND:COLS, :]) * scale
+        col0 = cols[0, row]
+        g_first = g_of(tap_near[row], col0, 0)
+        far = grads[:BAND].astype(BF).astype(F32)
+        gr[row, 0:BAND, :] = (mm_tn(g_first, fl[row, 0:BAND, :]) * scale + far).astype(BF)
+        near = grads[BAND:]
+        first = mm(g_first, fr[row, 0:BAND, :])
 
         if row < FWD:
-            g_back = g_of(tap_near[row], spread(row, 0), BAND)
+            g_back = g_of(tap_near[row], col0, BAND)
             gl[row, 0:BAND, :] = ((first + mm(g_back, prev[row])) * scale).astype(BF)
             near1[row] = near
         else:
@@ -501,6 +499,23 @@
         finish_send(spec)
 
 
+def hand_on(*refs):
+    half = len(refs) // 2
+    for src, dst in zip(refs[:half], refs[half:]):
+        dst[...] = src[...]
+
+
+def whole_copy(*arrays):
+    specs = [pl.BlockSpec((4,) + a.shape[1:], lambda i: (i, 0, 0)) for a in arrays]
+    return pl.pallas_call(
+        hand_on,
+        grid=(ROWS // 4,),
+        out_shape=tuple(jax.ShapeDtypeStruct(a.shape, a.dtype) for a in arrays),
+        in_specs=specs,
+        out_specs=tuple(specs),
+    )(*arrays)
+
+
 def per_device(n_rows, n_cols, feat_left, feat_right, hidden, disparity, motion_weight, gate_weight, cand_weight, grad_hidden):
     taps = motion_weight.shape[0]
     feat = feat_left.shape[2]
@@ -509,7 +524,7 @@
     hbm = pl.BlockSpec(memory_space=pl.ANY)
     vmem = pl.BlockSpec(memory_space=pltpu.VMEM)
     v = pltpu.VMEM
-    return pl.pallas_call(
+    outs = pl.pallas_call(
         functools.partial(kernel, n_rows, n_cols, taps, 1.0 / math.sqrt(feat)),
         out_shape=(
             jax.ShapeDtypeStruct(hidden.shape, BF),
@@ -532,6 +547,7 @@
             v((2, BWD, TAP_PAD, BAND), BF),
             v((ROWS, BAND, feat), F32),
             v((ROWS, BAND, BAND), F32),
+            v((2, ROWS, BAND, BAND), jnp.int32),
             v((ROWS, 1, COLS), jnp.int32),
             v((BAND, CH), BF),
             v((EXT, WIDE, CH), BF),
@@ -560,6 +576,7 @@
         ),
         cost_estimate=pl.CostEstimate(flops=17 * 10**9, bytes_accessed=14 * 10**6, transcendentals=0),
     )(feat_left, feat_right, hidden, grad_hidden, wg, wc, disparity, motion_weight)
+    return whole_copy(*outs)
 
 
 def solution(mesh):

time: 91.2 us -> 83.9 us (0.920)
  local copies, waits for them, and re-layouts: 6.11 us -> 0 us
  Pallas kernels: 84.2 us -> 82.9 us
    pallas_call x1, Pallas kernels: 84.2 us -> 77.7 us  [per_device(): pl.pallas_call(functools.partial(kernel, n_rows, n_cols, taps, 1.0 / math...]
    unnamed x7 -> x0, local copies, waits for them, and re-layouts: 6.11 us -> none
    pallas_call x0 -> x1, Pallas kernels: none -> 5.26 us  [whole_copy(): pl.pallas_call(hand_on, grid=(ROWS // 4,), out_shape=tuple((jax.ShapeDtyp...]
where the time goes in v4:
time: 83.9 us; the launch traced here: 83.6 us
  Pallas kernels  82.9 us (99%)
    pallas_call x1, Pallas kernels, per_device(): pl.pallas_call(functools.partial(kernel, n_rows, n_cols, taps, 1.0 / math...  77.7 us
    pallas_call x1, Pallas kernels, whole_copy(): pl.pallas_call(hand_on, grid=(ROWS // 4,), out_shape=tuple((jax.ShapeDtyp...  5.26 us

profile of v4, /device:TPU:12, one launch (start us, length us, event | category | flops | bytes accessed | tf_op | source)
XLA Modules:
  0.0 83.6 jit_solution(6467643958208579765)
XLA Ops:
  0.6 77.7 %shard_map.103 = (bf16[16,256,128]{2,1,0:T(8,128)(2,1)}, bf16[16,256,256]{2,1,0:T(8,128)(2,1)}, bf16[16,256,256]{2,1,0:T(8,128)(2,1)}) custom-call(bf16[16,256,256]{2,1,0:T(8,128)(2,1)} %fl_hbm.1, bf16[16,256,256]{2,1,0:T(8,128)(2,1)} %fr_hbm.1, bf16[16,256,128]{2,1,0:T(8,128)(2,1)} %hid_hbm.1, bf16[16,256,128]{2,1,0:T(8,128)(2,1)} %g_hbm.1, ...), custom_call_target="tpu_custom_call" | custom-call | flops 16999999488 | bytes 14000000 | tf_op jit(solution)/shard_map/pallas_call | solution.py:527
  78.3 5.3 %shard_map.104 = (bf16[16,256,128]{2,1,0:T(8,128)(2,1)}, bf16[16,256,256]{2,1,0:T(8,128)(2,1)}, bf16[16,256,256]{2,1,0:T(8,128)(2,1)}) custom-call(bf16[16,256,128]{2,1,0:T(8,128)(2,1)} %get-tuple-element.6.refs_0_, bf16[16,256,256]{2,1,0:T(8,128)(2,1)} %get-tuple-element.7.refs_1_, bf16[16,256,256]{2,1,0:T(8,128)(2,1)} %get-tuple-element.8.refs_2_), custom_call_target="tpu_custom_call" | custom-call | tf_op jit(solution)/shard_map/pallas_call | solution.py:510

commit v5 on v4

--- a/solution.py
+++ b/solution.py
@@ -353,9 +353,7 @@
         return ref[pl.ds(r, count)].reshape(count * WIDE, ref.shape[2])
 
     def gate_pair(r):
-        acc = mm(rows_of(in3, r - 1, 2), wg[0:768, :])
-        acc = acc + mm(rows_of(in3, r, 2), wg[768:1536, :])
-        acc = acc + mm(rows_of(in3, r + 1, 2), wg[1536:2304, :])
+        acc = mm(jnp.concatenate([rows_of(in3, r + a, 2) for a in (-1, 0, 1)], axis=1), wg[...])
         for s in range(2):
             part = acc[s * WIDE : (s + 1) * WIDE]
             reset = sig(part[:, CH:])
@@ -398,9 +396,7 @@
 
     def back_pair(n):
         r = HALO - 1 + 2 * n
-        acc = mm(rows_of(cg3, r - 1, 2), wct[0:384, :])
-        acc = acc + mm(rows_of(cg3, r - 2, 2), wct[384:768, :])
-        acc = acc + mm(rows_of(cg3, r - 3, 2), wct[768:1152, :])
+        acc = mm(jnp.concatenate([rows_of(cg3, r - a, 2) for a in (1, 2, 3)], axis=1), wct[...])
         for s in range(2):
             part = acc[s * WIDE : (s + 1) * WIDE]
             reset = rst[r + s - 1]

time: 83.9 us -> 83.5 us (level)
  no operation moved by 1% of the time
where the time goes in v5:
time: 83.5 us; the launch traced here: 83.2 us
  Pallas kernels  82.6 us (99%)
    pallas_call x1, Pallas kernels, per_device(): pl.pallas_call(functools.partial(kernel, n_rows, n_cols, taps, 1.0 / math...  77.3 us
    pallas_call x1, Pallas kernels, whole_copy(): pl.pallas_call(hand_on, grid=(ROWS // 4,), out_shape=tuple((jax.ShapeDtyp...  5.26 us

profile of v5, /device:TPU:12, one launch (start us, length us, event | category | flops | bytes accessed | tf_op | source)
XLA Modules:
  0.0 83.2 jit_solution(2011525886946525419)
XLA Ops:
  0.6 77.3 %shard_map.103 = (bf16[16,256,128]{2,1,0:T(8,128)(2,1)}, bf16[16,256,256]{2,1,0:T(8,128)(2,1)}, bf16[16,256,256]{2,1,0:T(8,128)(2,1)}) custom-call(bf16[16,256,256]{2,1,0:T(8,128)(2,1)} %fl_hbm.1, bf16[16,256,256]{2,1,0:T(8,128)(2,1)} %fr_hbm.1, bf16[16,256,128]{2,1,0:T(8,128)(2,1)} %hid_hbm.1, bf16[16,256,128]{2,1,0:T(8,128)(2,1)} %g_hbm.1, ...), custom_call_target="tpu_custom_call" | custom-call | flops 16999999488 | bytes 14000000 | tf_op jit(solution)/shard_map/pallas_call | solution.py:523
  78.0 5.3 %shard_map.104 = (bf16[16,256,128]{2,1,0:T(8,128)(2,1)}, bf16[16,256,256]{2,1,0:T(8,128)(2,1)}, bf16[16,256,256]{2,1,0:T(8,128)(2,1)}) custom-call(bf16[16,256,128]{2,1,0:T(8,128)(2,1)} %get-tuple-element.6.refs_0_, bf16[16,256,256]{2,1,0:T(8,128)(2,1)} %get-tuple-element.7.refs_1_, bf16[16,256,256]{2,1,0:T(8,128)(2,1)} %get-tuple-element.8.refs_2_), custom_call_target="tpu_custom_call" | custom-call | tf_op jit(solution)/shard_map/pallas_call | solution.py:506
